TPU v7x, 512 devices: a whole 4x4x16 slice. The times are simulated.
512 devices in a mesh: tm: 64 (over x, z), mp: 8 (over y, core).
Axes of the slice: x: 4, y: 4, z: 16, core: 2. Of those that a mesh axis runs over, the one named last changes fastest.
Arguments:
- observations: bfloat16 [64, 4096, 256], P('tm', None, 'mp'), may hold values from -6 to 6
- contact: int32 [512, 8, 8], P('tm'), may hold values 0 or 1
- resets: int32 [8, 4096], P(None, 'tm'), may hold values 0 or 1
- q_weight: bfloat16 [2048, 1024], P(None, 'mp'), may hold values from -0.125 to 0.125
- k_weight: bfloat16 [2048, 1024], P(None, 'mp'), may hold values from -0.125 to 0.125
- v_weight: bfloat16 [2048, 1024], P(None, 'mp'), may hold values from -0.125 to 0.125
- decay_weight: bfloat16 [2048, 1024], P(None, 'mp'), may hold values from -0.125 to 0.125
- gate_weight: bfloat16 [2048, 1024], P(None, 'mp'), may hold values from -0.125 to 0.125
- decay_bias: float32 [8, 128], P('mp'), may hold values from 4 to 14
- norm_gain: float32 [8, 128], P('mp'), may hold values from 0.25 to 1.75
- out_weight: bfloat16 [1024, 2048], P(None, 'mp'), may hold values from -0.1875 to 0.1875
- out_cotangent: bfloat16 [8, 4096, 2048], P(None, 'tm', 'mp'), may hold values from -0.03125 to 0.03125
Outputs:
- following_frame: bfloat16 [8, 4096, 2048], P(None, 'tm', 'mp')
- out_weight_grad: float32 [1024, 2048], P('tm', 'mp')
All inputs are finite; a program needn't handle non-finite values. No bound on the sum of `contact` or of `resets` on one device may be relied on, other than what follows from the above.
Results may differ from a plain program's by a relative error of at most 0.0049.
Values may be sent and summed in bfloat16 or wider, within the bound.
A program may use at most 128 MiB of HBM per device.

v0:
```python
import jax
import jax.numpy as jnp
from jax import lax
from jax.sharding import PartitionSpec as P

HK = 128
CH = 8


def prefix(part, axis, combine, identity):
    place = lax.axis_index(axis)
    gathered = jax.tree.map(lambda a: lax.all_gather(a, axis), part)
    state = jax.tree.map(lambda a, e: jnp.zeros_like(a) + jnp.asarray(e, a.dtype), part, identity)

    def one(hop, state):
        return combine(
            state, jax.tree.map(lambda a: lax.dynamic_index_in_dim(a, hop, 0, False), gathered)
        )

    return lax.fori_loop(0, place, one, state)


def block_terms(queries, key_rows, value_rows, log_decay, reset_block):
    frames = queries.shape[2]
    log_total = jnp.cumsum(log_decay, axis=2)
    resets_observed = jnp.cumsum(reset_block, axis=1)
    last_total = log_total[:, :, -1, :]
    last_seen = resets_observed[:, -1]
    untouched = (resets_observed == 0).astype(jnp.float32)[:, None, :, None]
    survives = (resets_observed == last_seen[:, None]).astype(jnp.float32)[:, None, :, None]
    block_decay = jnp.exp(last_total) * (last_seen == 0).astype(jnp.float32)[:, None, None]
    weights = jnp.exp(last_total[:, :, None, :] - log_total) * survives
    block_state = jnp.einsum(
        "chtk,chtv->chkv", key_rows * weights, value_rows, precision=lax.Precision.HIGHEST
    )
    carried_q = queries * jnp.exp(log_total) * untouched
    middle = log_total[:, :, frames // 2 : frames // 2 + 1, :]
    scaled_q = queries * jnp.exp(log_total - middle)
    scaled_k = key_rows * jnp.exp(middle - log_total)
    scores = jnp.einsum("chtk,chsk->chts", scaled_q, scaled_k, precision=lax.Precision.HIGHEST)
    row_index = lax.broadcasted_iota(jnp.int32, (frames, frames), 0)
    earlier = lax.broadcasted_iota(jnp.int32, (frames, frames), 1)
    causal = (row_index >= earlier)[None, :, :] & (
        resets_observed[:, :, None] == resets_observed[:, None, :]
    )
    scores = jnp.where(causal[:, None, :, :], scores, 0.0)
    inside = jnp.einsum("chts,chsv->chtv", scores, value_rows, precision=lax.Precision.HIGHEST)
    return (block_decay, block_state, carried_q, inside)


def finish(attended, gate_values, gain_head, links_block):
    characters, head_count, frames, value_width = attended.shape
    blocks = links_block.shape[0]
    mean_square = jnp.mean(attended * attended, axis=-1, keepdims=True)
    normed = attended * lax.rsqrt(mean_square + 1e-06) * gain_head[None, :, None, :]
    normed = normed.transpose(0, 2, 1, 3).reshape(characters, frames, head_count * value_width)
    regrouped_rows = normed.reshape(characters, blocks, frames // blocks * head_count * value_width)
    contact_factor = links_block.astype(jnp.float32)
    total_rows = jnp.einsum(
        "nmr,rnd->mnd", contact_factor, regrouped_rows, precision=lax.Precision.HIGHEST
    )
    partners = jnp.maximum(jnp.sum(contact_factor, axis=-1), 1.0)
    mixed_rows = regrouped_rows + total_rows / jnp.transpose(partners)[:, :, None]
    mixed_rows = mixed_rows.reshape(characters, frames, head_count * value_width)
    return (mixed_rows * jax.nn.silu(gate_values)).astype(jnp.bfloat16)


def combine_states(earlier, later_part):
    return (earlier[0] * later_part[0], later_part[0][..., None] * earlier[1] + later_part[1])


def local(
    observations,
    contact,
    resets,
    q_weight,
    k_weight,
    v_weight,
    decay_weight,
    gate_weight,
    decay_bias,
    norm_gain,
    out_weight,
    out_cotangent,
):
    span_time = lax.axis_size("tm")
    splits = span_time // CH
    characters = resets.shape[0]
    frames = resets.shape[1]
    head_count = decay_bias.shape[0]
    matrices = (q_weight, k_weight, v_weight, decay_weight, gate_weight)
    zero_sums = tuple(
        (jnp.zeros((characters, frames, matrix.shape[1]), jnp.float32) for matrix in matrices)
    )
    full_rows = lax.all_gather(observations, "mp", axis=2, tiled=True)
    rollout = lax.all_to_all(full_rows, "tm", split_axis=1, concat_axis=0, tiled=True)
    span_width = rollout.shape[2]
    regrouped_rows = rollout.reshape(characters, splits, frames, span_width)
    result = []
    for partial_sum, matrix in zip(zero_sums, matrices):
        blocked = matrix.reshape(splits, matrix.shape[0] // splits, matrix.shape[1])
        result.append(
            jnp.einsum("cgtf,gfh->cth", regrouped_rows, blocked, preferred_element_type=jnp.float32)
        )
    projected = tuple(result)

    def head_major(values):
        return values.reshape(characters, frames, head_count, -1).transpose(0, 2, 1, 3)

    queries = head_major(projected[0] * HK ** (-0.5))
    key_rows = head_major(projected[1])
    value_rows = head_major(projected[2])
    log_decay = head_major(
        jax.nn.log_sigmoid(projected[3].reshape(characters, frames, head_count, -1) + decay_bias)
    )
    block_decay, block_state, carried_q, inside = block_terms(
        queries, key_rows, value_rows, log_decay, resets
    )
    identity = (jnp.ones_like(block_decay), jnp.zeros_like(block_state))
    entering = prefix((block_decay, block_state), "tm", combine_states, identity)
    attended = inside + jnp.einsum(
        "chtk,chkv->chtv", carried_q, entering[1], precision=lax.Precision.HIGHEST
    )
    gated = finish(attended, projected[4], norm_gain, contact)
    gated_rows = gated.reshape(characters * frames, -1)
    cotangent_rows = out_cotangent.reshape(characters * frames, -1)
    portion = lax.all_gather(gated_rows, "mp", axis=1, tiled=True)
    produced = jnp.dot(portion, out_weight, preferred_element_type=jnp.float32)
    gradient_piece = lax.dot_general(
        portion, cotangent_rows, (((0,), (0,)), ((), ())), preferred_element_type=jnp.float32
    )
    produced, partial_grad = (produced, gradient_piece)
    following_frame = produced.astype(jnp.bfloat16).reshape(characters, frames, -1)
    weight_grad = lax.psum_scatter(partial_grad, "tm", scatter_dimension=0, tiled=True)
    return (following_frame, weight_grad)


def solution(mesh):
    placed = (
        P("tm", None, "mp"),
        P("tm", None, None),
        P(None, "tm"),
        P(None, "mp"),
        P(None, "mp"),
        P(None, "mp"),
        P(None, "mp"),
        P(None, "mp"),
        P("mp", None),
        P("mp", None),
        P(None, "mp"),
        P(None, "tm", "mp"),
    )
    return jax.shard_map(
        local,
        mesh=mesh,
        in_specs=placed,
        out_specs=(P(None, "tm", "mp"), P("tm", "mp")),
        check_vma=False,
    )
```

profile of v0, /device:TPU:8, one launch (start us, length us, event | category | flops | bytes accessed | tf_op | source)
XLA Modules:
  0.0 1353.7 jit_solution(6704598011931905069)
XLA Ops:
  7.2 0.7 all-gather.5.cloned.1.call-update
  7.9 38.6 %all-gather.5.cloned.1.call-done = bf16[1,4096,256]{1,2,0:T(8,128)(2,1)} async-done(((bf16[1,4096,32]{1,2,0:T(8,128)(2,1)}), bf16[1,4096,256]{1,2,0:T(8,128)(2,1)}) %all-gather.5.cloned.1.call-update) | async-done | bytes 2097168 | tf_op jit(solution)/shard_map/all_gather | solution.py:95
  46.5 10.0 copy.41
  56.5 0.5 broadcast.79
  57.0 21.6 %reduce.4 = bf16[4096,256]{1,0:T(8,128)(2,1)S(1)} reduce(bf16[4096,1,256]{2,1,0:T(2,128)(2,1)} %bitcast.127, bf16[]{:T(256)} %broadcast.79), dimensions={1}, to_apply=%bitcast.99.reduce_sub_computation | reduce | bytes 4194306
  78.6 2.1 reshape.229
  80.7 15.7 %all-to-all-start = ((bf16[64,2,8192]{2,1,0:T(2,128)(2,1)}), bf16[64,2,8192]{2,1,0:T(2,128)(2,1)S(1)}, u32[]{:S(2)}, u32[]{:S(2)}) async-start(bf16[64,2,8192]{2,1,0:T(2,128)(2,1)} %reshape.229), calls=%async_computation | async-start | bytes 4194304 | tf_op jit(solution)/shard_map/all_to_all | solution.py:96
  96.5 0.2 reduce_window_sum.24
  96.7 0.2 slice_reduce_fusion
  97.0 97.4 %all-to-all-done = bf16[64,2,8192]{2,1,0:T(2,128)(2,1)S(1)} async-done(((bf16[64,2,8192]{2,1,0:T(2,128)(2,1)}), bf16[64,2,8192]{2,1,0:T(2,128)(2,1)S(1)}, u32[]{:S(2)}, u32[]{:S(2)}) %all-to-all-start) | async-done | bytes 2097184 | tf_op jit(solution)/shard_map/all_to_all | solution.py:96
  194.4 6.7 reshape.230
  201.1 2.5 copy.53
  203.7 0.7 convolution_bitcast_fusion.2
  204.4 0.3 copy-done.7
  204.7 0.8 fusion.7
  205.5 0.2 fusion.23
  205.7 0.7 convolution_bitcast_fusion.1
  206.4 1.9 fusion.20
  208.6 87.3 %all_gather.17 = f32[64,8,1,128]{3,1,2,0:T(8,128)} all-gather(f32[1,8,1,128]{3,1,2,0:T(8,128)S(1)} %bitcast_multiply_fusion), channel_id=1, replica_groups=mesh['tm'=64,'mp'=8] {'tm'}, dimensions={0}, use_global_device_ids=true | all-gather | bytes 266240 | tf_op jit(solution)/shard_map/all_gather | solution.py:12
  295.9 1.9 fusion
  297.9 0.7 copy-done.1
  298.6 0.6 convolution_select_fusion
  299.2 1.1 fusion.33
  300.3 196.3 %all-gather.9.cloned.1.call-done = f32[512,128,128]{2,1,0:T(8,128)} async-done(((f32[8,128,128]{2,1,0:T(8,128)}), f32[512,128,128]{2,1,0:T(8,128)}) %all-gather.9.cloned.1.call-update) | async-done | bytes 33554448 | tf_op jit(solution)/shard_map/all_gather | solution.py:12
  496.6 0.2 while.12
  496.8 1.8 multiply_reduce_fusion
  498.8 0.6 fusion.2
  499.6 2.5 multiply_convert_fusion
  502.1 147.1 %all-gather.7.cloned.1.call-done = bf16[512,1024]{1,0:T(8,128)(2,1)} async-done(((bf16[512,128]{1,0:T(8,128)(2,1)}), bf16[512,1024]{1,0:T(8,128)(2,1)}) %all-gather.7.cloned.1.call-update) | async-done | bytes 1048592 | tf_op jit(solution)/shard_map/all_gather | solution.py:127
  649.2 2.8 fusion.34
  652.1 1.1 convolution_convert_fusion
  653.2 693.9 %reduce-scatter.2.cloned.1.call-done = f32[16,256]{1,0:T(8,128)} async-done(((f32[1024,256]{1,0:T(8,128)}), f32[16,256]{1,0:T(8,128)}) %reduce-scatter.2.cloned.1.call-update) | async-done | bytes 16400 | tf_op jit(solution)/shard_map/reduce_scatter | solution.py:134
  (40 shorter events, 1.0 us)
Async XLA Ops:
  7.2 196.5 %copy-start = (bf16[2048,128]{1,0:T(8,128)(2,1)S(1)}, bf16[2048,128]{1,0:T(8,128)(2,1)}, u32[]{:S(2)}) copy-start(bf16[2048,128]{1,0:T(8,128)(2,1)} %param.18) | copy-start | bytes 1572868
  7.2 39.3 %all-gather.5.cloned.1.call-start = ((), (), s32[]{:S(2)}) async-start(), calls=%async_computation.2 | async-start | bytes 2359296 | tf_op jit(solution)/shard_map/all_gather | solution.py:95
  80.7 15.8 %copy-start.5 = (s32[8,64]{1,0:T(8,128)S(1)}, s32[8,64]{1,0:T(8,128)}, u32[]{:S(2)}) copy-start(s32[8,64]{1,0:T(8,128)} %param.16) | copy-start | bytes 6148
  80.7 113.6 %all-to-all-start = ((bf16[64,2,8192]{2,1,0:T(2,128)(2,1)}), bf16[64,2,8192]{2,1,0:T(2,128)(2,1)S(1)}, u32[]{:S(2)}, u32[]{:S(2)}) async-start(bf16[64,2,8192]{2,1,0:T(2,128)(2,1)} %reshape.229), calls=%async_computation | async-start | bytes 4194304 | tf_op jit(solution)/shard_map/all_to_all | solution.py:96
  96.5 400.1 %all-gather.9.cloned.1.call-start = ((), (), s32[]{:S(2)}) async-start(), calls=%async_computation.5 | async-start | bytes 34078720 | tf_op jit(solution)/shard_map/all_gather | solution.py:12
  203.6 1.0 copy-start.7
  203.7 1.0 copy-start.10
  204.7 1.0 copy-start.8
  205.7 2.7 copy-start.4
  208.4 440.8 %all-gather.7.cloned.1.call-start = ((), (), s32[]{:S(2)}) async-start(), calls=%async_computation.3 | async-start | bytes 1179648 | tf_op jit(solution)/shard_map/all_gather | solution.py:127
  297.8 0.7 copy-start.1
  496.6 2.0 copy-start.6
  499.6 149.7 %copy-start.3 = (bf16[8,64,256]{2,1,0:T(8,128)(2,1)S(1)}, bf16[8,64,256]{2,1,0:T(8,128)(2,1)}, u32[]{:S(2)}) copy-start(bf16[8,64,256]{2,1,0:T(8,128)(2,1)} %param.25) | copy-start | bytes 786436
  502.1 150.0 %copy-start.9 = (bf16[1024,256]{1,0:T(8,128)(2,1)S(1)}, bf16[1024,256]{1,0:T(8,128)(2,1)}, u32[]{:S(2)}) copy-start(bf16[1024,256]{1,0:T(8,128)(2,1)} %param.24) | copy-start | bytes 1572868
  502.1 845.1 %reduce-scatter.2.cloned.1.call-start = ((), (), s32[]{:S(2)}) async-start(), calls=%async_computation.4 | async-start | bytes 1064960 | tf_op jit(solution)/shard_map/reduce_scatter | solution.py:134
  649.2 2.9 copy-start.2
Sparse Core Ops, SparseCore 0:
  10.2 36.2 all-gather.4
  208.5 287.9 all-gather.8
  502.2 146.9 all-gather.6
  654.0 693.0 reduce-scatter.1
where the time goes:
time: 1360 us; the launch traced here: 1350 us
  waiting for transfers between devices  1170 us (86%)
  blocking collectives  87.3 us (6%)
  local copies, waits for them, and re-layouts  23.5 us (2%)
  other arithmetic  22.3 us (2%)
  matrix products  16.5 us (1%)
  starting transfers between devices  15.9 us (1%)
  between operations  14 us (1%)
    reduce_scatter x1, waiting for transfers between devices, local(): lax.psum_scatter(partial_grad, 'tm', scatter_dimension=0, tiled=True)  694 us
    all_gather x1, waiting for transfers between devices, prefix(): gathered = jax.tree.map(lambda a: lax.all_gather(a, axis), part)  196 us
    all_gather x1, waiting for transfers between devices, local(): portion = lax.all_gather(gated_rows, 'mp', axis=1, tiled=True)  147 us
    all_to_all x1, waiting for transfers between devices, local(): lax.all_to_all(full_rows, 'tm', split_axis=1, concat_axis=0, tiled=True)  97.4 us
    all_gather x1, blocking collectives, prefix(): gathered = jax.tree.map(lambda a: lax.all_gather(a, axis), part)  87.3 us
    all_gather x1, waiting for transfers between devices, local(): full_rows = lax.all_gather(observations, 'mp', axis=2, tiled=True)  38.6 us
  transfers between devices with their start and end apart: 5, of which 5 were waited for; matrix products, arithmetic and copies ran while one was open for 0% of the time, Pallas kernels for 0%

commit v1 on v0

v1 whole, which is shorter than its diff:
```python
import jax
import jax.numpy as jnp
from jax import lax
from jax.experimental import pallas as pl
from jax.experimental.pallas import tpu as pltpu
from jax.sharding import PartitionSpec as P

MESH = pl.DeviceIdType.MESH
BF = jnp.bfloat16
F32 = jnp.float32

HK = 128
CH = 8
TM, MP = 64, 8
NX, NZ, NY = 4, 16, 4
FR = 64
ROWS = CH * FR
LEVELS = (32, 16, 8, 4, 2, 1)


def dot(a, b, dims=((1,), (0,))):
    return lax.dot_general(a, b, (dims, ((), ())), preferred_element_type=F32)


def split(a):
    high = a.astype(BF)
    return high, (a - high.astype(F32)).astype(BF)


def dot3(a, b, dims=((1,), (0,))):
    ah, al = split(a)
    bh, bl = split(b)
    da, db = dims[0][0], dims[1][0]
    return dot(jnp.concatenate([ah, al, ah], da), jnp.concatenate([bh, bh, bl], db), dims)


def iota(shape, dim):
    return lax.broadcasted_iota(jnp.int32, shape, dim)


def kernel(
    obs, contact, resets, wq, wk, wv, wd, wg, bias, gain, ow, cot,
    out, grad,
    obs_v, con_v, res_v, w_v, bias_v, gain_v, ow_v, cot_v,
    pack, rx, feat, proj, decay_log, rcol, rrow, masks, sel, mix, inv_partners,
    sbuf, dbuf, st_in, d_in, d_t, pre, s_in, attended, carried_q, silu,
    gat, oacc, gradf, gbuf, xr, zf, zbuf, zr, out_v, grad_v,
    in_sem, w_sem, out_sem, a_sem, f_send, f_recv, st_sem, dk_sem, p_sem, g_send, g_recv, x_sem, z_sem,
):
    T = lax.axis_index("tm")
    M = lax.axis_index("mp")
    x, z = T // NZ, lax.rem(T, NZ)
    y, core = M // 2, lax.rem(M, 2)
    right_y, left_y, opp_y = lax.rem(y + 1, NY), lax.rem(y + 3, NY), lax.rem(y + 2, NY)

    def load(src, dst, i):
        return pltpu.make_async_copy(src, dst, in_sem.at[i])

    loads = [
        load(obs, obs_v, 0), load(contact, con_v, 1), load(resets, res_v, 2), load(bias, bias_v, 3),
        load(gain, gain_v, 4), load(ow, ow_v, 5), load(cot, cot_v, 6),
    ]
    loads[0].start()

    barrier = pltpu.get_barrier_semaphore()

    @pl.loop(1, TM)
    def _(k):
        pl.semaphore_signal(barrier, inc=1, device_id=(lax.rem(T + k, TM), M), device_id_type=MESH)

    sib = 2 * y + 1 - core
    right, left, opp = 2 * right_y + core, 2 * left_y + core, 2 * opp_y + core
    for other in (sib, right, left):
        pl.semaphore_signal(barrier, inc=1, device_id=(T, other), device_id_type=MESH)

    for one in loads[1:]:
        one.start()

    @pl.loop(0, MP)
    def _(m):
        for j, w in enumerate((wq, wk, wv, wd, wg)):
            for fh in range(2):
                pltpu.make_async_copy(
                    w.at[:, m, fh], w_v.at[m, fh, :, :, pl.ds(j * 128, 128)], w_sem
                ).start()

    loads[0].wait()
    low = iota((16, 128), 1) < 64

    @pl.loop(0, TM // 2)
    def _(u):
        tile = obs_v[:, pl.ds(pl.multiple_of(u * 128, 128), 128)].astype(F32)
        a, b = tile[:16], tile[16:]
        pack[2 * u] = jnp.where(low, a, pltpu.roll(b, 64, 1)).astype(BF)
        pack[2 * u + 1] = jnp.where(low, pltpu.roll(a, 64, 1), b).astype(BF)

    pl.semaphore_wait(barrier, TM - 1 + 3)

    def piece(src, dst, sems, peer):
        return pltpu.make_async_remote_copy(
            src_ref=src, dst_ref=dst, send_sem=sems.at[0], recv_sem=sems.at[1],
            device_id=(peer, M), device_id_type=MESH,
        )

    def wait_bytes(ref, sem):
        pltpu.make_async_copy(ref, ref, sem).wait()

    @pl.loop(1, TM)
    def _(k):
        peer = lax.rem(T + k, TM)
        piece(pack.at[peer], rx.at[T], a_sem, peer).start()

    rx[T] = pack[T]

    for one in loads[1:]:
        one.wait()
    tri = (iota((FR, FR), 0) >= iota((FR, FR), 1)).astype(BF)
    res = res_v[...].astype(F32).astype(BF)
    seen_col = dot(tri, res, ((1,), (1,)))
    seen_row = dot(res, tri, ((1,), (1,)))
    for c in range(CH):
        rcol[c] = jnp.broadcast_to(seen_col[:, c : c + 1], (FR, 128))
        rrow[c] = seen_row[c : c + 1, :]
    t_id, s_id = iota((FR, FR), 0), iota((FR, FR), 1)
    for i, h in enumerate(LEVELS):
        masks[i] = ((t_id // (2 * h) == s_id // (2 * h)) & (t_id // h > s_id // h)).astype(F32)
        sel[i * FR : (i + 1) * FR] = (s_id == (t_id // (2 * h)) * (2 * h) + h - 1).astype(BF)
    masks[len(LEVELS)] = (t_id == s_id).astype(F32)

    row_q, col_q = iota((ROWS, FR), 0), iota((ROWS, FR), 1)
    pick = (((row_q % FR) // 8) * 8 + row_q // FR == col_q).astype(BF)
    con = con_v[...].astype(F32).astype(BF)
    taken = dot(pick, con).astype(BF)
    inv_partners[...] = 1.0 / jnp.maximum(dot(taken, jnp.ones((CH, 128), BF)), 1.0)
    spread = (iota((CH, ROWS), 1) // FR == iota((CH, ROWS), 0)).astype(BF)
    same = iota((ROWS, ROWS), 0) % FR == iota((ROWS, ROWS), 1) % FR
    mix[...] = jnp.where(same, dot(taken, spread), 0.0).astype(BF)

    wait_bytes(rx.at[pl.ds(0, TM - 1)], a_sem.at[1])
    for c in range(CH):
        turned = rx[c * 8 : (c + 1) * 8].reshape(128, 128).T
        feat[M, c * FR : (c + 1) * FR, 0:128] = turned[:FR]
        feat[M, c * FR : (c + 1) * FR, 128:256] = turned[FR:]

    def gather(buf, send, recv, use):
        half = ROWS // 2

        def part(slot, h, i, to):
            ref = buf.at[slot, pl.ds(h * half, half)]
            return pltpu.make_async_remote_copy(
                src_ref=ref, dst_ref=ref, send_sem=send.at[i], recv_sem=recv.at[i],
                device_id=(T, to), device_id_type=MESH,
            )

        sent = []

        def go(*args):
            one = part(*args)
            one.start()
            sent.append(one)

        def arrived(slot, h, i):
            part(slot, h, i, sib).wait_recv()

        go(M, 0, 2, right)
        go(M, 1, 5, left)
        go(M, 0, 0, sib)
        go(M, 1, 1, sib)
        go(M, 1, 3, right)
        go(M, 0, 4, left)
        use(M, True)
        arrived(left, 0, 2)
        go(left, 0, 6, right)
        go(left, 0, 8, sib)
        arrived(right, 1, 5)
        go(right, 1, 7, left)
        go(right, 1, 11, sib)
        arrived(sib, 0, 0)
        arrived(sib, 1, 1)
        use(sib, False)
        arrived(left, 1, 3)
        go(left, 1, 9, sib)
        arrived(right, 0, 4)
        go(right, 0, 10, sib)
        use(left, False)
        use(right, False)
        arrived(opp, 0, 6)
        go(opp, 0, 12, sib)
        arrived(opp, 1, 7)
        go(opp, 1, 13, sib)
        use(opp, False)
        for yy, i in ((left_y, 8), (right_y, 10), (opp_y, 12)):
            slot = 2 * yy + 1 - core
            arrived(slot, 0, i)
            arrived(slot, 1, i + 1)
            use(slot, False)
        return sent

    wait_bytes(w_v, w_sem)

    def project(m, first):
        term = dot(feat[m], w_v[m].reshape(256, 640))
        proj[...] = term if first else proj[...] + term

    pending = gather(feat, f_send, f_recv, project)

    bias_row, gain_row = bias_v[...], gain_v[...]
    mine_c, mine_k = T // 8, lax.rem(T, 8)

    @pl.loop(0, CH)
    def _(i):
        c = lax.rem(mine_c + i, CH)
        rows = pl.ds(pl.multiple_of(c * FR, FR), FR)
        logit = proj[rows, 384:512] + bias_row
        u = jnp.exp(-jnp.abs(logit))
        log1p = jnp.where(u < 1e-3, u * (1.0 - 0.5 * u), jnp.log(1.0 + u))
        log_decay = jnp.minimum(logit, 0.0) - log1p
        both = dot(tri, jnp.concatenate(split(log_decay), 1))
        total = both[:, :128] + both[:, 128:]
        decay_log[rows, :] = total
        seen = rcol[c]
        last, last_seen = total[FR - 1 :], seen[FR - 1 :]
        weight = jnp.where(seen == last_seen, jnp.exp(jnp.minimum(last - total, 0.0)), 0.0)
        state = dot3(proj[rows, 128:256] * weight, proj[rows, 256:384], ((0,), (0,)))
        sbuf[pl.ds(pl.multiple_of(c * 8, 8), 8)] = state.astype(BF).reshape(8, 16, 128)
        dbuf[c] = jnp.where(last_seen == 0.0, jnp.exp(last), 0.0)

        @pl.loop(0, 8)
        def _(n):
            peer = c * 8 + lax.rem(mine_k + n, 8)

            @pl.when(peer != T)
            def _():
                piece(dbuf.at[c], d_in.at[T], dk_sem, peer).start()
                piece(sbuf.at[peer], st_in.at[T], st_sem, peer).start()

    d_in[T] = dbuf[mine_c]
    st_in[T] = sbuf[T]

    @pl.loop(0, CH)
    def _(c):
        rows = pl.ds(pl.multiple_of(c * FR, FR), FR)
        total = decay_log[rows, :]
        queries = proj[rows, 0:128] * HK ** (-0.5)
        keys, values = proj[rows, 128:256], proj[rows, 256:384]
        seen = rcol[c]
        carried_q[rows, :] = jnp.where(seen == 0.0, queries * jnp.exp(total), 0.0)
        picked = dot(sel[...], jnp.concatenate(split(total), 1))
        picked = picked[:, :128] + picked[:, 128:]
        scores = masks[len(LEVELS)] * dot3(queries, keys, ((1,), (1,)))
        for i in range(len(LEVELS)):
            gap = jnp.exp(-jnp.abs(total - picked[i * FR : (i + 1) * FR]))
            scores += masks[i] * dot3(queries * gap, keys * gap, ((1,), (1,)))
        scores = jnp.where(seen[:, :FR] == rrow[c], scores, 0.0)
        attended[rows, :] = dot3(scores, values)
        gate = proj[rows, 512:640]
        silu[rows, :] = gate / (1.0 + jnp.exp(-gate))

    wait_bytes(d_in.at[pl.ds(0, TM - 1)], dk_sem.at[1])
    wait_bytes(st_in.at[pl.ds(0, TM - 1)], st_sem.at[1])
    d_t[...] = d_in[...].reshape(TM, 128).T
    decays = d_t[pl.ds(pl.multiple_of(mine_k * 16, 16), 16), :]
    state = jnp.zeros((16, 128), F32)
    for t in range(TM):
        pre[t] = state.astype(BF)
        if t < TM - 1:
            state = state * decays[:, t : t + 1] + st_in[t].astype(F32)

    @pl.loop(1, TM)
    def _(k):
        peer = lax.rem(T + k, TM)
        piece(pre.at[peer], s_in.at[T], p_sem, peer).start()

    s_in[T] = pre[T]
    wait_bytes(s_in.at[pl.ds(0, TM - 1)], p_sem.at[1])

    @pl.loop(0, CH)
    def _(c):
        rows = pl.ds(pl.multiple_of(c * FR, FR), FR)
        entering = s_in[pl.ds(pl.multiple_of(c * 8, 8), 8)].reshape(128, 128)
        q2 = jnp.concatenate(split(carried_q[rows, :]), 1)
        full = attended[rows, :] + dot(q2, jnp.concatenate([entering, entering], 0))
        square = jnp.mean(full * full, axis=-1, keepdims=True)
        attended[rows, :] = full * lax.rsqrt(square + 1e-06) * gain_row

    normed = attended[...]
    mixed = dot(mix[...], jnp.concatenate(split(normed), 1))
    blended = normed + (mixed[:, :128] + mixed[:, 128:]) * inv_partners[...]
    gat[M] = (blended * silu[...]).astype(BF)

    def produce(m, first):
        rows = gat[m]
        term = dot(rows, ow_v[m])
        oacc[...] = term if first else oacc[...] + term
        part = dot(rows, cot_v[...], ((0,), (0,))).reshape(8, 16, 256)
        gradf[m] = part
        gbuf[m] = part.astype(BF)

    pending += gather(gat, g_send, g_recv, produce)

    def along_x(d):
        to = lax.rem(x + d, NX)
        return piece(gbuf.at[pl.ds(2 * to, 2)], xr.at[x], x_sem, to * NZ + z)

    across = [along_x(d) for d in (2, 1, 3)]
    for one in across:
        one.start()
    out_v[...] = oacc[...].astype(BF)
    store = pltpu.make_async_copy(out_v, out, out_sem.at[0])
    store.start()

    wait_bytes(xr.at[pl.ds(0, NX - 1)], x_sem.at[1])
    total = gradf[pl.ds(2 * x, 2)]
    for d in range(1, NX):
        total += xr[lax.rem(x + d, NX)].astype(F32)
    total = total.reshape(NZ, 16, 256)
    zf[...] = total
    zbuf[...] = total.astype(BF)

    @pl.loop(1, NZ)
    def _(k):
        to = lax.rem(z + k, NZ)
        piece(zbuf.at[to], zr.at[z], z_sem, x * NZ + to).start()

    wait_bytes(zr.at[pl.ds(0, NZ - 1)], z_sem.at[1])
    total = zf[z]
    for k in range(1, NZ):
        total += zr[lax.rem(z + k, NZ)].astype(F32)
    grad_v[...] = total
    last_store = pltpu.make_async_copy(grad_v, grad, out_sem.at[1])
    last_store.start()

    wait_bytes(pack.at[pl.ds(0, TM - 1)], a_sem.at[0])
    for one in pending:
        one.wait_send()
    wait_bytes(d_in.at[pl.ds(0, TM - 1)], dk_sem.at[0])
    wait_bytes(sbuf.at[pl.ds(0, TM - 1)], st_sem.at[0])
    wait_bytes(pre.at[pl.ds(0, TM - 1)], p_sem.at[0])
    wait_bytes(xr.at[pl.ds(0, NX - 1)], x_sem.at[0])
    wait_bytes(zbuf.at[pl.ds(0, NZ - 1)], z_sem.at[0])
    store.wait()
    last_store.wait()


def local(
    observations, contact, resets, q_weight, k_weight, v_weight, decay_weight, gate_weight,
    decay_bias, norm_gain, out_weight, out_cotangent,
):
    features = jnp.swapaxes(observations[0], 0, 1)
    weights = [
        w.reshape(8, MP, 2, 16, 128) for w in (q_weight, k_weight, v_weight, decay_weight, gate_weight)
    ]
    vm = pltpu.VMEM
    dma = pltpu.SemaphoreType.DMA
    scratch = [
        vm((32, 4096), BF), vm((FR, CH), jnp.int32), vm((CH, FR), jnp.int32),
        vm((MP, 2, 8, 16, 640), BF), vm((1, 128), F32), vm((1, 128), F32),
        vm((MP, 128, 256), BF), vm((ROWS, 256), BF),
        vm((TM, 16, 128), BF), vm((TM, 16, 128), BF), vm((MP, ROWS, 256), BF),
        vm((ROWS, 640), F32), vm((ROWS, 128), F32), vm((CH, FR, 128), F32), vm((CH, 1, FR), F32),
        vm((len(LEVELS) + 1, FR, FR), F32), vm((len(LEVELS) * FR, FR), BF),
        vm((ROWS, ROWS), BF), vm((ROWS, 128), F32),
        vm((TM, 16, 128), BF), vm((CH, 1, 128), F32), vm((TM, 16, 128), BF), vm((TM, 1, 128), F32),
        vm((128, TM), F32), vm((TM, 16, 128), BF), vm((TM, 16, 128), BF),
        vm((ROWS, 128), F32), vm((ROWS, 128), F32), vm((ROWS, 128), F32),
        vm((MP, ROWS, 128), BF), vm((ROWS, 256), F32), vm((MP, 8, 16, 256), F32),
        vm((MP, 8, 16, 256), BF), vm((NX, 2, 8, 16, 256), BF), vm((NZ, 16, 256), F32),
        vm((NZ, 16, 256), BF), vm((NZ, 16, 256), BF), vm((ROWS, 256), BF), vm((16, 256), F32),
        dma((7,)), dma, dma((2,)), dma((2,)), dma((14,)), dma((14,)), dma((2,)), dma((2,)), dma((2,)),
        dma((14,)), dma((14,)), dma((2,)), dma((2,)),
    ]
    following, weight_grad = pl.pallas_call(
        kernel,
        out_shape=(
            jax.ShapeDtypeStruct((ROWS, 256), BF),
            jax.ShapeDtypeStruct((16, 256), F32),
        ),
        in_specs=[pl.BlockSpec(memory_space=pl.ANY)] * 12,
        out_specs=(pl.BlockSpec(memory_space=pl.ANY),) * 2,
        scratch_shapes=scratch,
        compiler_params=pltpu.CompilerParams(
            collective_id=0, has_side_effects=True, vmem_limit_bytes=40 * 2**20
        ),
    )(
        features, contact.reshape(FR, CH), resets, *weights, decay_bias, norm_gain,
        out_weight.reshape(MP, 128, 256), out_cotangent.reshape(ROWS, 256),
    )
    return following.reshape(CH, FR, 256), weight_grad


def solution(mesh):
    placed = (
        P("tm", None, "mp"),
        P("tm", None, None),
        P(None, "tm"),
        P(None, "mp"),
        P(None, "mp"),
        P(None, "mp"),
        P(None, "mp"),
        P(None, "mp"),
        P("mp", None),
        P("mp", None),
        P(None, "mp"),
        P(None, "tm", "mp"),
    )
    return jax.shard_map(
        local,
        mesh=mesh,
        in_specs=placed,
        out_specs=(P(None, "tm", "mp"), P("tm", "mp")),
        check_vma=False,
    )
```

time: 1360 us -> 124 us (0.09)
  waiting for transfers between devices: 1170 us -> 0 us
  Pallas kernels: 0 us -> 112 us
  blocking collectives: 87.3 us -> 0 us
  other arithmetic: 22.3 us -> 0 us
  matrix products: 16.5 us -> 0 us
  starting transfers between devices: 15.9 us -> 0 us
    reduce_scatter x1 -> x0, waiting for transfers between devices: 694 us -> none  [local(): lax.psum_scatter(partial_grad, 'tm', scatter_dimension=0, tiled=True)]
    all_gather x3 -> x0, waiting for transfers between devices: 382 us -> none  [the longest x1 196 us: prefix(): gathered = jax.tree.map(lambda a: lax.all_gather(a, axis), part)]
    pallas_call x0 -> x1, Pallas kernels: none -> 112 us  [local(): pl.pallas_call(kernel, out_shape=(jax.ShapeDtypeStruct((ROWS, 256), BF),...]
    all_to_all x1 -> x0, waiting for transfers between devices: 97.4 us -> none  [local(): lax.all_to_all(full_rows, 'tm', split_axis=1, concat_axis=0, tiled=True)]
    all_gather x1 -> x0, blocking collectives: 87.3 us -> none  [prefix(): gathered = jax.tree.map(lambda a: lax.all_gather(a, axis), part)]
    unnamed x1 -> x0, other arithmetic: 21.6 us -> none
    dot_general x12 -> x0, matrix products: 16.5 us -> none  [the longest x5 6.54 us: local(): jnp.einsum('cgtf,gfh->cth', regrouped_rows, blocked, preferred_element_ty...]
    all_to_all x1 -> x0, starting transfers between devices: 15.7 us -> none  [local(): lax.all_to_all(full_rows, 'tm', split_axis=1, concat_axis=0, tiled=True)]
  transfers between devices with their start and end apart: 5 -> 0, of which waited for: 5 -> 0; matrix products, arithmetic and copies ran while one was open for 0% -> 0% of each run, Pallas kernels for 0% -> 0%
where the time goes in v1:
time: 124 us; the launch traced here: 123 us
  Pallas kernels  112 us (90%)
  local copies, waits for them, and re-layouts  10.9 us (9%)
    pallas_call x1, Pallas kernels, local(): pl.pallas_call(kernel, out_shape=(jax.ShapeDtypeStruct((ROWS, 256), BF),...  112 us
    unnamed x26, local copies, waits for them, and re-layouts  10.9 us

profile of v1, /device:TPU:8, one launch (start us, length us, event | category | flops | bytes accessed | tf_op | source)
XLA Modules:
  0.0 123.3 jit_solution(9086347984496218102)
XLA Ops:
  0.6 0.0 copy-start.9
  0.6 0.0 copy-start.10
  0.7 0.0 copy-start.11
  0.7 0.7 copy-done.9
  1.3 0.0 copy-done.10
  1.3 0.0 copy-done.11
  1.3 0.0 copy-start
  1.3 1.0 copy-done
  2.4 0.0 copy-start.1
  2.4 1.0 copy-done.1
  3.4 0.0 copy-start.2
  3.4 1.0 copy-done.2
  4.5 0.0 copy-start.3
  4.5 1.0 copy-done.3
  5.5 0.0 copy-start.4
  5.5 1.0 copy-done.4
  6.5 0.0 copy-start.5
  6.5 1.0 copy-done.5
  7.6 0.0 copy-start.6
  7.6 0.9 copy-done.6
  8.5 0.0 copy-start.7
  8.5 0.9 copy-done.7
  9.5 0.0 copy-start.8
  9.5 0.8 copy-done.8
  10.2 111.8 %shard_map.131 = (bf16[512,256]{1,0:T(8,128)(2,1)S(1)}, f32[16,256]{1,0:T(8,128)S(1)}) custom-call(bf16[32,4096]{1,0:T(8,128)(2,1)S(1)} %bitcast.18, s32[64,8]{1,0:T(8,128)S(1)} %bitcast.21, s32[8,64]{1,0:T(8,128)S(1)} %copy-done.9, bf16[8,8,2,16,128]{4,3,2,1,0:T(8,128)(2,1)S(1)} %bitcast.12, bf16[8,8,2,16,128]{4,3,2,1,0:T(8,128)(2,1)S(1)} %bitcast.13, ...), custom_call_target="tpu_custom_call" | custom-call | tf_op jit(solution)/shard_map/pallas_call | solution.py:372
  122.0 0.7 copy.16
  122.7 0.6 copy.17
Async XLA Ops:
  0.6 0.7 copy-start.9
  0.6 0.7 copy-start.10
  0.7 0.7 copy-start.11
  1.3 1.0 copy-start
  2.4 1.0 copy-start.1
  3.4 1.0 copy-start.2
  4.5 1.0 copy-start.3
  5.5 1.0 copy-start.4
  6.5 1.0 copy-start.5
  7.6 0.9 copy-start.6
  8.5 0.9 copy-start.7
  9.5 0.8 copy-start.8

commit v2 on v1

--- a/solution.py
+++ b/solution.py
@@ -45,7 +45,7 @@
     pack, rx, feat, proj, decay_log, rcol, rrow, masks, sel, mix, inv_partners,
     sbuf, dbuf, st_in, d_in, d_t, pre, s_in, attended, carried_q, silu,
     gat, oacc, gradf, gbuf, xr, zf, zbuf, zr, out_v, grad_v,
-    in_sem, w_sem, out_sem, a_sem, f_send, f_recv, st_sem, dk_sem, p_sem, g_send, g_recv, x_sem, z_sem,
+    in_sem, w_sem, out_sem, a_send, a_recv, f_send, f_recv, st_sem, dk_sem, p_send, p_recv, g_send, g_recv, x_sem, z_sem,
 ):
     T = lax.axis_index("tm")
     M = lax.axis_index("mp")
@@ -105,10 +105,25 @@
     def wait_bytes(ref, sem):
         pltpu.make_async_copy(ref, ref, sem).wait()
 
-    @pl.loop(1, TM)
-    def _(k):
-        peer = lax.rem(T + k, TM)
-        piece(pack.at[peer], rx.at[T], a_sem, peer).start()
+    def piece_of_wave(src, dst, send, recv, d, peer):
+        return pltpu.make_async_remote_copy(
+            src_ref=src, dst_ref=dst, send_sem=send, recv_sem=recv.at[d],
+            device_id=(peer, M), device_id_type=MESH,
+        )
+
+    def to_wave(src, dst, send, recv, d):
+        @pl.loop(1 if d == 0 else 0, NZ)
+        def _(k):
+            peer = lax.rem(x + d, NX) * NZ + lax.rem(z + k, NZ)
+            piece_of_wave(src.at[peer], dst.at[T], send, recv, d, peer).start()
+
+    def from_wave(dst, recv, d):
+        wait_bytes(dst.at[pl.ds(0, NZ - 1 if d == 0 else NZ)], recv.at[d])
+
+    source = [lax.rem(x + NX - d, NX) for d in range(NX)]
+
+    for d in range(NX):
+        to_wave(pack, rx, a_send, a_recv, d)
 
     rx[T] = pack[T]
 
@@ -136,104 +151,109 @@
     same = iota((ROWS, ROWS), 0) % FR == iota((ROWS, ROWS), 1) % FR
     mix[...] = jnp.where(same, dot(taken, spread), 0.0).astype(BF)
 
-    wait_bytes(rx.at[pl.ds(0, TM - 1)], a_sem.at[1])
-    for c in range(CH):
-        turned = rx[c * 8 : (c + 1) * 8].reshape(128, 128).T
-        feat[M, c * FR : (c + 1) * FR, 0:128] = turned[:FR]
-        feat[M, c * FR : (c + 1) * FR, 128:256] = turned[FR:]
-
-    def gather(buf, send, recv, use):
-        half = ROWS // 2
-
-        def part(slot, h, i, to):
-            ref = buf.at[slot, pl.ds(h * half, half)]
-            return pltpu.make_async_remote_copy(
-                src_ref=ref, dst_ref=ref, send_sem=send.at[i], recv_sem=recv.at[i],
-                device_id=(T, to), device_id_type=MESH,
-            )
-
-        sent = []
-
-        def go(*args):
-            one = part(*args)
-            one.start()
-            sent.append(one)
-
-        def arrived(slot, h, i):
-            part(slot, h, i, sib).wait_recv()
-
-        go(M, 0, 2, right)
-        go(M, 1, 5, left)
-        go(M, 0, 0, sib)
-        go(M, 1, 1, sib)
-        go(M, 1, 3, right)
-        go(M, 0, 4, left)
-        use(M, True)
-        arrived(left, 0, 2)
-        go(left, 0, 6, right)
-        go(left, 0, 8, sib)
-        arrived(right, 1, 5)
-        go(right, 1, 7, left)
-        go(right, 1, 11, sib)
-        arrived(sib, 0, 0)
-        arrived(sib, 1, 1)
-        use(sib, False)
-        arrived(left, 1, 3)
-        go(left, 1, 9, sib)
-        arrived(right, 0, 4)
-        go(right, 0, 10, sib)
-        use(left, False)
-        use(right, False)
-        arrived(opp, 0, 6)
-        go(opp, 0, 12, sib)
-        arrived(opp, 1, 7)
-        go(opp, 1, 13, sib)
-        use(opp, False)
-        for yy, i in ((left_y, 8), (right_y, 10), (opp_y, 12)):
-            slot = 2 * yy + 1 - core
-            arrived(slot, 0, i)
-            arrived(slot, 1, i + 1)
-            use(slot, False)
-        return sent
-
     wait_bytes(w_v, w_sem)
-
-    def project(m, first):
-        term = dot(feat[m], w_v[m].reshape(256, 640))
-        proj[...] = term if first else proj[...] + term
-
-    pending = gather(feat, f_send, f_recv, project)
-
     bias_row, gain_row = bias_v[...], gain_v[...]
     mine_c, mine_k = T // 8, lax.rem(T, 8)
-
-    @pl.loop(0, CH)
-    def _(i):
-        c = lax.rem(mine_c + i, CH)
-        rows = pl.ds(pl.multiple_of(c * FR, FR), FR)
-        logit = proj[rows, 384:512] + bias_row
-        u = jnp.exp(-jnp.abs(logit))
-        log1p = jnp.where(u < 1e-3, u * (1.0 - 0.5 * u), jnp.log(1.0 + u))
-        log_decay = jnp.minimum(logit, 0.0) - log1p
-        both = dot(tri, jnp.concatenate(split(log_decay), 1))
-        total = both[:, :128] + both[:, 128:]
-        decay_log[rows, :] = total
-        seen = rcol[c]
-        last, last_seen = total[FR - 1 :], seen[FR - 1 :]
-        weight = jnp.where(seen == last_seen, jnp.exp(jnp.minimum(last - total, 0.0)), 0.0)
-        state = dot3(proj[rows, 128:256] * weight, proj[rows, 256:384], ((0,), (0,)))
-        sbuf[pl.ds(pl.multiple_of(c * 8, 8), 8)] = state.astype(BF).reshape(8, 16, 128)
-        dbuf[c] = jnp.where(last_seen == 0.0, jnp.exp(last), 0.0)
-
-        @pl.loop(0, 8)
-        def _(n):
-            peer = c * 8 + lax.rem(mine_k + n, 8)
-
-            @pl.when(peer != T)
-            def _():
-                piece(dbuf.at[c], d_in.at[T], dk_sem, peer).start()
-                piece(sbuf.at[peer], st_in.at[T], st_sem, peer).start()
-
+    pending = []
+
+    def send(one):
+        one.start()
+        pending.append(one)
+
+    def wave_rows(d):
+        return pl.ds(pl.multiple_of(source[d] * 2 * FR, 2 * FR), 2 * FR)
+
+    def part(d, slot, i, to):
+        ref = feat.at[slot, wave_rows(d)]
+        return pltpu.make_async_remote_copy(
+            src_ref=ref, dst_ref=ref, send_sem=f_send.at[d, i], recv_sem=f_recv.at[d, i],
+            device_id=(T, to), device_id_type=MESH,
+        )
+
+    def own_features(d):
+        from_wave(rx, a_recv, d)
+        for c in range(2):
+            tiles = rx[pl.ds(pl.multiple_of(source[d] * NZ + c * 8, 8), 8)]
+            turned = tiles.reshape(128, 128).T
+            rows = pl.ds(pl.multiple_of((source[d] * 2 + c) * FR, FR), FR)
+            feat[M, rows, 0:128] = turned[:FR]
+            feat[M, rows, 128:256] = turned[FR:]
+        send(part(d, M, 1, right))
+        send(part(d, M, 2, left))
+        send(part(d, M, 0, sib))
+
+    def pass_on(d):
+        for slot, i, to in ((left, 1, right), (right, 2, left)) if d % 2 == 0 else ((right, 2, left), (left, 1, right)):
+            part(d, slot, i, sib).wait_recv()
+            if (i == 1) == (d % 2 == 0):
+                send(part(d, slot, 3, to))
+            send(part(d, slot, 3 + i, sib))
+
+    def pass_opposite(d):
+        part(d, opp, 3, sib).wait_recv()
+        send(part(d, opp, 6, sib))
+
+    def add_projections(d, slots, first):
+        rows = wave_rows(d)
+        total = None if first else proj[rows, :]
+        for slot in slots:
+            term = dot(feat[slot, rows], w_v[slot].reshape(256, 640))
+            total = term if total is None else total + term
+        proj[rows, :] = total
+
+    def project(d):
+        part(d, sib, 0, sib).wait_recv()
+        add_projections(d, (M, left, right, opp, sib), True)
+        others = [2 * yy + 1 - core for yy in (left_y, right_y, opp_y)]
+        for slot, i in zip(others, (4, 5, 6)):
+            part(d, slot, i, sib).wait_recv()
+        add_projections(d, others, False)
+
+    def states(d):
+        for n in range(2):
+            c = source[d] * 2 + n
+            rows = pl.ds(pl.multiple_of(c * FR, FR), FR)
+            logit = proj[rows, 384:512] + bias_row
+            u = jnp.exp(-jnp.abs(logit))
+            log1p = jnp.where(u < 1e-3, u * (1.0 - 0.5 * u), jnp.log(1.0 + u))
+            log_decay = jnp.minimum(logit, 0.0) - log1p
+            both = dot(tri, jnp.concatenate(split(log_decay), 1))
+            total = both[:, :128] + both[:, 128:]
+            decay_log[rows, :] = total
+            seen = rcol[c]
+            last, last_seen = total[FR - 1 :], seen[FR - 1 :]
+            weight = jnp.where(seen == last_seen, jnp.exp(jnp.minimum(last - total, 0.0)), 0.0)
+            state = dot3(proj[rows, 128:256] * weight, proj[rows, 256:384], ((0,), (0,)))
+            sbuf[pl.ds(pl.multiple_of(c * 8, 8), 8)] = state.astype(BF).reshape(8, 16, 128)
+            dbuf[c] = jnp.where(last_seen == 0.0, jnp.exp(last), 0.0)
+
+        @pl.loop(1 if d == 0 else 0, NZ)
+        def _(k):
+            to = lax.rem(z + k, NZ)
+            peer = source[d] * NZ + to
+            piece(dbuf.at[source[d] * 2 + to // 8], d_in.at[T], dk_sem, peer).start()
+            piece(sbuf.at[peer], st_in.at[T], st_sem, peer).start()
+
+    own_features(0)
+    own_features(1)
+    pass_on(0)
+    pass_opposite(0)
+    project(0)
+    states(0)
+    own_features(2)
+    pass_on(1)
+    pass_opposite(1)
+    project(1)
+    states(1)
+    own_features(3)
+    pass_on(2)
+    pass_opposite(2)
+    pass_on(3)
+    project(2)
+    states(2)
+    pass_opposite(3)
+    project(3)
+    states(3)
     d_in[T] = dbuf[mine_c]
     st_in[T] = sbuf[T]
 
@@ -266,29 +286,42 @@
         if t < TM - 1:
             state = state * decays[:, t : t + 1] + st_in[t].astype(F32)
 
-    @pl.loop(1, TM)
-    def _(k):
-        peer = lax.rem(T + k, TM)
-        piece(pre.at[peer], s_in.at[T], p_sem, peer).start()
+    for d in range(NX):
+        to_wave(pre, s_in, p_send, p_recv, d)
 
     s_in[T] = pre[T]
-    wait_bytes(s_in.at[pl.ds(0, TM - 1)], p_sem.at[1])
-
-    @pl.loop(0, CH)
-    def _(c):
-        rows = pl.ds(pl.multiple_of(c * FR, FR), FR)
-        entering = s_in[pl.ds(pl.multiple_of(c * 8, 8), 8)].reshape(128, 128)
-        q2 = jnp.concatenate(split(carried_q[rows, :]), 1)
-        full = attended[rows, :] + dot(q2, jnp.concatenate([entering, entering], 0))
-        square = jnp.mean(full * full, axis=-1, keepdims=True)
-        attended[rows, :] = full * lax.rsqrt(square + 1e-06) * gain_row
+    for d in range(NX):
+        from_wave(s_in, p_recv, d)
+        for n in range(2):
+            c = source[d] * 2 + n
+            rows = pl.ds(pl.multiple_of(c * FR, FR), FR)
+            entering = s_in[pl.ds(pl.multiple_of(c * 8, 8), 8)].reshape(128, 128)
+            q2 = jnp.concatenate(split(carried_q[rows, :]), 1)
+            full = attended[rows, :] + dot(q2, jnp.concatenate([entering, entering], 0))
+            square = jnp.mean(full * full, axis=-1, keepdims=True)
+            attended[rows, :] = full * lax.rsqrt(square + 1e-06) * gain_row
 
     normed = attended[...]
     mixed = dot(mix[...], jnp.concatenate(split(normed), 1))
     blended = normed + (mixed[:, :128] + mixed[:, 128:]) * inv_partners[...]
     gat[M] = (blended * silu[...]).astype(BF)
 
-    def produce(m, first):
+    half = ROWS // 2
+
+    def gated_part(slot, h, i, to):
+        ref = gat.at[slot, pl.ds(h * half, half)]
+        return pltpu.make_async_remote_copy(
+            src_ref=ref, dst_ref=ref, send_sem=g_send.at[i], recv_sem=g_recv.at[i],
+            device_id=(T, to), device_id_type=MESH,
+        )
+
+    def go(*args):
+        send(gated_part(*args))
+
+    def arrived(slot, h, i):
+        gated_part(slot, h, i, sib).wait_recv()
+
+    def produce(m, first=False):
         rows = gat[m]
         term = dot(rows, ow_v[m])
         oacc[...] = term if first else oacc[...] + term
@@ -296,15 +329,47 @@
         gradf[m] = part
         gbuf[m] = part.astype(BF)
 
-    pending += gather(gat, g_send, g_recv, produce)
-
-    def along_x(d):
-        to = lax.rem(x + d, NX)
-        return piece(gbuf.at[pl.ds(2 * to, 2)], xr.at[x], x_sem, to * NZ + z)
-
-    across = [along_x(d) for d in (2, 1, 3)]
-    for one in across:
-        one.start()
+    def along_x(to):
+        @pl.when(to != x)
+        def _():
+            piece(gbuf.at[pl.ds(2 * to, 2)], xr.at[x], x_sem, to * NZ + z).start()
+
+    go(M, 0, 2, right)
+    go(M, 1, 5, left)
+    go(M, 0, 0, sib)
+    go(M, 1, 1, sib)
+    go(M, 1, 3, right)
+    go(M, 0, 4, left)
+    produce(M, True)
+    arrived(left, 0, 2)
+    go(left, 0, 6, right)
+    go(left, 0, 8, sib)
+    arrived(right, 1, 5)
+    go(right, 1, 7, left)
+    go(right, 1, 11, sib)
+    arrived(sib, 0, 0)
+    arrived(sib, 1, 1)
+    produce(sib)
+    along_x(y)
+    arrived(left, 1, 3)
+    go(left, 1, 9, sib)
+    arrived(right, 0, 4)
+    go(right, 0, 10, sib)
+    produce(left)
+    arrived(opp, 0, 6)
+    go(opp, 0, 12, sib)
+    arrived(opp, 1, 7)
+    go(opp, 1, 13, sib)
+    produce(right)
+    for yy, i in ((left_y, 8), (right_y, 10), (opp_y, 12)):
+        slot = 2 * yy + 1 - core
+        arrived(slot, 0, i)
+        arrived(slot, 1, i + 1)
+        if i == 12:
+            produce(opp)
+        produce(slot)
+        along_x(yy)
+
     out_v[...] = oacc[...].astype(BF)
     store = pltpu.make_async_copy(out_v, out, out_sem.at[0])
     store.start()
@@ -330,12 +395,12 @@
     last_store = pltpu.make_async_copy(grad_v, grad, out_sem.at[1])
     last_store.start()
 
-    wait_bytes(pack.at[pl.ds(0, TM - 1)], a_sem.at[0])
+    wait_bytes(pack.at[pl.ds(0, TM - 1)], a_send)
     for one in pending:
         one.wait_send()
     wait_bytes(d_in.at[pl.ds(0, TM - 1)], dk_sem.at[0])
     wait_bytes(sbuf.at[pl.ds(0, TM - 1)], st_sem.at[0])
-    wait_bytes(pre.at[pl.ds(0, TM - 1)], p_sem.at[0])
+    wait_bytes(pre.at[pl.ds(0, TM - 1)], p_send)
     wait_bytes(xr.at[pl.ds(0, NX - 1)], x_sem.at[0])
     wait_bytes(zbuf.at[pl.ds(0, NZ - 1)], z_sem.at[0])
     store.wait()
@@ -366,7 +431,7 @@
         vm((MP, ROWS, 128), BF), vm((ROWS, 256), F32), vm((MP, 8, 16, 256), F32),
         vm((MP, 8, 16, 256), BF), vm((NX, 2, 8, 16, 256), BF), vm((NZ, 16, 256), F32),
         vm((NZ, 16, 256), BF), vm((NZ, 16, 256), BF), vm((ROWS, 256), BF), vm((16, 256), F32),
-        dma((7,)), dma, dma((2,)), dma((2,)), dma((14,)), dma((14,)), dma((2,)), dma((2,)), dma((2,)),
+        dma((7,)), dma, dma((2,)), dma, dma((NX,)), dma((NX, 7)), dma((NX, 7)), dma((2,)), dma((2,)), dma, dma((NX,)),
         dma((14,)), dma((14,)), dma((2,)), dma((2,)),
     ]
     following, weight_grad = pl.pallas_call(
@@ -375,11 +440,11 @@
             jax.ShapeDtypeStruct((ROWS, 256), BF),
             jax.ShapeDtypeStruct((16, 256), F32),
         ),
-        in_specs=[pl.BlockSpec(memory_space=pl.ANY)] * 12,
-        out_specs=(pl.BlockSpec(memory_space=pl.ANY),) * 2,
+        in_specs=[pl.BlockSpec(memory_space=pltpu.HBM)] * 12,
+        out_specs=(pl.BlockSpec(memory_space=pltpu.HBM),) * 2,
         scratch_shapes=scratch,
         compiler_params=pltpu.CompilerParams(
-            collective_id=0, has_side_effects=True, vmem_limit_bytes=40 * 2**20
+            collective_id=0, has_side_effects=True, vmem_limit_bytes=60 * 2**20
         ),
     )(
         features, contact.reshape(FR, CH), resets, *weights, decay_bias, norm_gain,

time: 124 us -> 115 us (0.927)
  the two profiles are of different devices: /device:TPU:8 before, /device:TPU:26 now
where the time goes in v2:
time: 115 us
  Pallas kernels  112 us (97%)
  local copies, waits for them, and re-layouts  2.28 us (2%)
    pallas_call x1, Pallas kernels, local(): pl.pallas_call(kernel, out_shape=(jax.ShapeDtypeStruct((ROWS, 256), BF),...  112 us

profile of v2, /device:TPU:26, one launch (start us, length us, event | category | flops | bytes accessed | tf_op | source)
XLA Modules:
  0.0 114.9 jit_solution(8881574007187030361)
XLA Ops:
  0.6 112.0 %shard_map.131 = (bf16[512,256]{1,0:T(8,128)(2,1)}, f32[16,256]{1,0:T(8,128)}) custom-call(bf16[32,4096]{1,0:T(8,128)(2,1)} %bitcast.18, s32[64,8]{1,0:T(8,128)} %bitcast.21, s32[8,64]{1,0:T(8,128)} %resets.1, bf16[8,8,2,16,128]{4,3,2,1,0:T(8,128)(2,1)} %bitcast.12, bf16[8,8,2,16,128]{4,3,2,1,0:T(8,128)(2,1)} %bitcast.13, ...), custom_call_target="tpu_custom_call" | custom-call | tf_op jit(solution)/shard_map/pallas_call | solution.py:437
  112.6 0.0 copy-start
  112.6 1.7 %copy.16 = bf16[8,64,256]{2,1,0:T(8,128)(2,1)} copy(bf16[8,64,256]{2,1,0:T(8,128)(2,1)} %bitcast.20) | data formatting | bytes 524288
  114.3 0.0 copy-done
  114.3 0.6 copy.17
Async XLA Ops:
  112.6 1.7 %copy-start = (f32[16,256]{1,0:T(8,128)S(1)}, f32[16,256]{1,0:T(8,128)}, u32[]{:S(2)}) copy-start(f32[16,256]{1,0:T(8,128)} %get-tuple-element.9) | copy-start | bytes 49156

commit v3 on v2

--- a/solution.py
+++ b/solution.py
@@ -16,6 +16,7 @@
 FR = 64
 ROWS = CH * FR
 LEVELS = (32, 16, 8, 4, 2, 1)
+WAVE = 2 * FR
 
 
 def dot(a, b, dims=((1,), (0,))):
@@ -38,27 +39,39 @@
     return lax.broadcasted_iota(jnp.int32, shape, dim)
 
 
+def column(row):
+    return jnp.broadcast_to(row, (8, 128)).T[:, :1]
+
+
 def kernel(
     obs, contact, resets, wq, wk, wv, wd, wg, bias, gain, ow, cot,
     out, grad,
-    obs_v, con_v, res_v, w_v, bias_v, gain_v, ow_v, cot_v,
-    pack, rx, feat, proj, decay_log, rcol, rrow, masks, sel, mix, inv_partners,
-    sbuf, dbuf, st_in, d_in, d_t, pre, s_in, attended, carried_q, silu,
+    con_v, res_v, w_v, bias_v, gain_v, ow_v, cot_v,
+    rx, feat, proj, decay_log, res_own, res_in, rcol, rrow, masks, sel, mix, inv_partners,
+    local_state, before, s_own, d_own, s_in, d_in, attended, carried_q,
+    gate_own, gate_in, norm_own, norm_in,
     gat, oacc, gradf, gbuf, xr, zf, zbuf, zr, out_v, grad_v,
-    in_sem, w_sem, out_sem, a_send, a_recv, f_send, f_recv, st_sem, dk_sem, p_send, p_recv, g_send, g_recv, x_sem, z_sem,
+    in_sem, w_sem, out_sem, a_send, a_recv, f_send, f_recv, r_sem, s_send, s_recv, d_send, d_recv,
+    gate_sem, norm_sem, g_send, g_recv, x_sem, z_sem,
 ):
     T = lax.axis_index("tm")
     M = lax.axis_index("mp")
     x, z = T // NZ, lax.rem(T, NZ)
     y, core = M // 2, lax.rem(M, 2)
+    span, place = T // CH, lax.rem(T, CH)
+    char = lax.rem(place + span, CH)
+
+    def holder(other_span, other_char):
+        return other_span * CH + lax.rem(other_char - other_span + CH, CH)
+
     right_y, left_y, opp_y = lax.rem(y + 1, NY), lax.rem(y + 3, NY), lax.rem(y + 2, NY)
 
     def load(src, dst, i):
         return pltpu.make_async_copy(src, dst, in_sem.at[i])
 
     loads = [
-        load(obs, obs_v, 0), load(contact, con_v, 1), load(resets, res_v, 2), load(bias, bias_v, 3),
-        load(gain, gain_v, 4), load(ow, ow_v, 5), load(cot, cot_v, 6),
+        load(resets, res_v, 0), load(contact, con_v, 1), load(bias, bias_v, 2),
+        load(gain, gain_v, 3), load(ow, ow_v, 4), load(cot, cot_v, 5),
     ]
     loads[0].start()
 
@@ -79,20 +92,14 @@
     @pl.loop(0, MP)
     def _(m):
         for j, w in enumerate((wq, wk, wv, wd, wg)):
-            for fh in range(2):
-                pltpu.make_async_copy(
-                    w.at[:, m, fh], w_v.at[m, fh, :, :, pl.ds(j * 128, 128)], w_sem
-                ).start()
+            pltpu.make_async_copy(w.at[:, m], w_v.at[m, :, :, pl.ds(j * 128, 128)], w_sem).start()
 
     loads[0].wait()
-    low = iota((16, 128), 1) < 64
-
-    @pl.loop(0, TM // 2)
-    def _(u):
-        tile = obs_v[:, pl.ds(pl.multiple_of(u * 128, 128), 128)].astype(F32)
-        a, b = tile[:16], tile[16:]
-        pack[2 * u] = jnp.where(low, a, pltpu.roll(b, 64, 1)).astype(BF)
-        pack[2 * u + 1] = jnp.where(low, pltpu.roll(a, 64, 1), b).astype(BF)
+    res = res_v[...].astype(F32)
+    res = jnp.concatenate([res, jnp.zeros_like(res)], 1)
+    for c in range(CH):
+        res_own[c] = res[c : c + 1]
+    res_in[place] = res_own[char]
 
     pl.semaphore_wait(barrier, TM - 1 + 3)
 
@@ -111,26 +118,36 @@
             device_id=(peer, M), device_id_type=MESH,
         )
 
-    def to_wave(src, dst, send, recv, d):
-        @pl.loop(1 if d == 0 else 0, NZ)
+    def quarter(to, d):
+        return obs.at[:, pl.ds(pl.multiple_of(to * CH * FR + d * WAVE, WAVE), WAVE)]
+
+    for d in range(NX):
+        @pl.loop(0, CH)
         def _(k):
-            peer = lax.rem(x + d, NX) * NZ + lax.rem(z + k, NZ)
-            piece_of_wave(src.at[peer], dst.at[T], send, recv, d, peer).start()
-
-    def from_wave(dst, recv, d):
-        wait_bytes(dst.at[pl.ds(0, NZ - 1 if d == 0 else NZ)], recv.at[d])
-
-    source = [lax.rem(x + NX - d, NX) for d in range(NX)]
-
-    for d in range(NX):
-        to_wave(pack, rx, a_send, a_recv, d)
-
-    rx[T] = pack[T]
+            to = lax.rem(span + k, CH)
+            peer = holder(to, span)
+
+            @pl.when(peer != T)
+            def _():
+                pltpu.make_async_remote_copy(
+                    src_ref=quarter(to, d), dst_ref=rx.at[d, place], send_sem=a_send, recv_sem=a_recv.at[d],
+                    device_id=(peer, M), device_id_type=MESH,
+                ).start()
+
+        @pl.when(place == 0)
+        def _():
+            pltpu.make_async_copy(quarter(span, d), rx.at[d, place], a_recv.at[d]).start()
+
+    @pl.loop(1, CH)
+    def _(k):
+        to = lax.rem(place + k, CH)
+        piece(res_own.at[lax.rem(to + span, CH)], res_in.at[place], r_sem, span * CH + to).start()
 
     for one in loads[1:]:
         one.wait()
     tri = (iota((FR, FR), 0) >= iota((FR, FR), 1)).astype(BF)
-    res = res_v[...].astype(F32).astype(BF)
+    wait_bytes(res_in.at[pl.ds(0, CH - 1)], r_sem.at[1])
+    res = res_in[...].reshape(CH, 128)[:, :FR].astype(BF)
     seen_col = dot(tri, res, ((1,), (1,)))
     seen_row = dot(res, tri, ((1,), (1,)))
     for c in range(CH):
@@ -149,11 +166,16 @@
     inv_partners[...] = 1.0 / jnp.maximum(dot(taken, jnp.ones((CH, 128), BF)), 1.0)
     spread = (iota((CH, ROWS), 1) // FR == iota((CH, ROWS), 0)).astype(BF)
     same = iota((ROWS, ROWS), 0) % FR == iota((ROWS, ROWS), 1) % FR
+    @pl.loop(0, CH)
+    def _(k):
+        @pl.when(k >= span)
+        def _():
+            s_in[k] = jnp.zeros((128, 128), BF)
+            d_in[k] = jnp.ones((1, 128), F32)
+
     mix[...] = jnp.where(same, dot(taken, spread), 0.0).astype(BF)
 
-    wait_bytes(w_v, w_sem)
     bias_row, gain_row = bias_v[...], gain_v[...]
-    mine_c, mine_k = T // 8, lax.rem(T, 8)
     pending = []
 
     def send(one):
@@ -161,7 +183,7 @@
         pending.append(one)
 
     def wave_rows(d):
-        return pl.ds(pl.multiple_of(source[d] * 2 * FR, 2 * FR), 2 * FR)
+        return pl.ds(d * WAVE, WAVE)
 
     def part(d, slot, i, to):
         ref = feat.at[slot, wave_rows(d)]
@@ -171,13 +193,8 @@
         )
 
     def own_features(d):
-        from_wave(rx, a_recv, d)
-        for c in range(2):
-            tiles = rx[pl.ds(pl.multiple_of(source[d] * NZ + c * 8, 8), 8)]
-            turned = tiles.reshape(128, 128).T
-            rows = pl.ds(pl.multiple_of((source[d] * 2 + c) * FR, FR), FR)
-            feat[M, rows, 0:128] = turned[:FR]
-            feat[M, rows, 128:256] = turned[FR:]
+        wait_bytes(rx.at[d], a_recv.at[d])
+        feat[M, wave_rows(d)] = rx[d].reshape(256, WAVE).T
         send(part(d, M, 1, right))
         send(part(d, M, 2, left))
         send(part(d, M, 0, sib))
@@ -192,6 +209,8 @@
     def pass_opposite(d):
         part(d, opp, 3, sib).wait_recv()
         send(part(d, opp, 6, sib))
+
+    wait_bytes(w_v, w_sem)
 
     def add_projections(d, slots, first):
         rows = wave_rows(d)
@@ -210,9 +229,8 @@
         add_projections(d, others, False)
 
     def states(d):
-        for n in range(2):
-            c = source[d] * 2 + n
-            rows = pl.ds(pl.multiple_of(c * FR, FR), FR)
+        for s in (2 * d, 2 * d + 1):
+            rows = pl.ds(s * FR, FR)
             logit = proj[rows, 384:512] + bias_row
             u = jnp.exp(-jnp.abs(logit))
             log1p = jnp.where(u < 1e-3, u * (1.0 - 0.5 * u), jnp.log(1.0 + u))
@@ -220,19 +238,32 @@
             both = dot(tri, jnp.concatenate(split(log_decay), 1))
             total = both[:, :128] + both[:, 128:]
             decay_log[rows, :] = total
-            seen = rcol[c]
+            seen = rcol[s]
             last, last_seen = total[FR - 1 :], seen[FR - 1 :]
             weight = jnp.where(seen == last_seen, jnp.exp(jnp.minimum(last - total, 0.0)), 0.0)
             state = dot3(proj[rows, 128:256] * weight, proj[rows, 256:384], ((0,), (0,)))
-            sbuf[pl.ds(pl.multiple_of(c * 8, 8), 8)] = state.astype(BF).reshape(8, 16, 128)
-            dbuf[c] = jnp.where(last_seen == 0.0, jnp.exp(last), 0.0)
-
-        @pl.loop(1 if d == 0 else 0, NZ)
-        def _(k):
-            to = lax.rem(z + k, NZ)
-            peer = source[d] * NZ + to
-            piece(dbuf.at[source[d] * 2 + to // 8], d_in.at[T], dk_sem, peer).start()
-            piece(sbuf.at[peer], st_in.at[T], st_sem, peer).start()
+            decay = jnp.where(last_seen == 0.0, jnp.exp(last), 0.0)
+            if s == 0:
+                before[0] = jnp.ones((1, 128), F32)
+                local_state[0] = jnp.zeros((128, 128), F32)
+                after, product = state, decay
+            else:
+                after = local_state[s] * column(decay) + state
+                product = before[s] * decay
+            if s < CH - 1:
+                local_state[s + 1] = after
+                before[s + 1] = product
+            else:
+                s_own[...] = after.astype(BF)
+                d_own[...] = product
+
+    def gates(d):
+        gate = proj[wave_rows(d), 512:640]
+        gate_own[wave_rows(d)] = gate / (1.0 + jnp.exp(-gate))
+        for s in (2 * d, 2 * d + 1):
+            @pl.when(s != place)
+            def _():
+                piece(gate_own.at[pl.ds(s * FR, FR)], gate_in.at[char], gate_sem, span * CH + s).start()
 
     own_features(0)
     own_features(1)
@@ -240,22 +271,51 @@
     pass_opposite(0)
     project(0)
     states(0)
+    gates(0)
     own_features(2)
     pass_on(1)
     pass_opposite(1)
     project(1)
     states(1)
+    gates(1)
     own_features(3)
     pass_on(2)
     pass_opposite(2)
     pass_on(3)
     project(2)
     states(2)
+    gates(2)
     pass_opposite(3)
     project(3)
     states(3)
-    d_in[T] = dbuf[mine_c]
-    st_in[T] = sbuf[T]
+
+    def to_span(k):
+        peer = holder(lax.rem(span + k, CH), char)
+        return [
+            pltpu.make_async_remote_copy(
+                src_ref=src, dst_ref=dst.at[span], send_sem=sent.at[k], recv_sem=recv.at[span],
+                device_id=(peer, M), device_id_type=MESH,
+            )
+            for src, dst, sent, recv in ((s_own, s_in, s_send, s_recv), (d_own, d_in, d_send, d_recv))
+        ]
+
+    for k in range(1, CH):
+        @pl.when(span + k < CH)
+        def _():
+            for one in to_span(k):
+                one.start()
+
+    def to_owners(src, dst, sems):
+        @pl.loop(1, CH)
+        def _(k):
+            to = lax.rem(place + k, CH)
+            rows = pl.ds(pl.multiple_of(to * FR, FR), FR)
+            piece(src.at[rows], dst.at[char], sems, span * CH + to).start()
+
+        dst[char] = src[pl.ds(pl.multiple_of(place * FR, FR), FR)]
+
+    gates(3)
+    gate_in[char] = gate_own[pl.ds(pl.multiple_of(place * FR, FR), FR)]
 
     @pl.loop(0, CH)
     def _(c):
@@ -264,7 +324,8 @@
         queries = proj[rows, 0:128] * HK ** (-0.5)
         keys, values = proj[rows, 128:256], proj[rows, 256:384]
         seen = rcol[c]
-        carried_q[rows, :] = jnp.where(seen == 0.0, queries * jnp.exp(total), 0.0)
+        carried = jnp.where(seen == 0.0, queries * jnp.exp(total), 0.0)
+        carried_q[rows, :] = carried * before[c]
         picked = dot(sel[...], jnp.concatenate(split(total), 1))
         picked = picked[:, :128] + picked[:, 128:]
         scores = masks[len(LEVELS)] * dot3(queries, keys, ((1,), (1,)))
@@ -272,39 +333,28 @@
             gap = jnp.exp(-jnp.abs(total - picked[i * FR : (i + 1) * FR]))
             scores += masks[i] * dot3(queries * gap, keys * gap, ((1,), (1,)))
         scores = jnp.where(seen[:, :FR] == rrow[c], scores, 0.0)
-        attended[rows, :] = dot3(scores, values)
-        gate = proj[rows, 512:640]
-        silu[rows, :] = gate / (1.0 + jnp.exp(-gate))
-
-    wait_bytes(d_in.at[pl.ds(0, TM - 1)], dk_sem.at[1])
-    wait_bytes(st_in.at[pl.ds(0, TM - 1)], st_sem.at[1])
-    d_t[...] = d_in[...].reshape(TM, 128).T
-    decays = d_t[pl.ds(pl.multiple_of(mine_k * 16, 16), 16), :]
-    state = jnp.zeros((16, 128), F32)
-    for t in range(TM):
-        pre[t] = state.astype(BF)
-        if t < TM - 1:
-            state = state * decays[:, t : t + 1] + st_in[t].astype(F32)
-
-    for d in range(NX):
-        to_wave(pre, s_in, p_send, p_recv, d)
-
-    s_in[T] = pre[T]
-    for d in range(NX):
-        from_wave(s_in, p_recv, d)
-        for n in range(2):
-            c = source[d] * 2 + n
-            rows = pl.ds(pl.multiple_of(c * FR, FR), FR)
-            entering = s_in[pl.ds(pl.multiple_of(c * 8, 8), 8)].reshape(128, 128)
-            q2 = jnp.concatenate(split(carried_q[rows, :]), 1)
-            full = attended[rows, :] + dot(q2, jnp.concatenate([entering, entering], 0))
-            square = jnp.mean(full * full, axis=-1, keepdims=True)
-            attended[rows, :] = full * lax.rsqrt(square + 1e-06) * gain_row
-
-    normed = attended[...]
-    mixed = dot(mix[...], jnp.concatenate(split(normed), 1))
-    blended = normed + (mixed[:, :128] + mixed[:, 128:]) * inv_partners[...]
-    gat[M] = (blended * silu[...]).astype(BF)
+        attended[rows, :] = dot3(scores, values) + dot3(carried, local_state[c])
+
+    for k in range(CH - 1):
+        @pl.when(k < span)
+        def _():
+            pltpu.make_async_copy(s_in.at[k], s_in.at[k], s_recv.at[k]).wait()
+            pltpu.make_async_copy(d_in.at[k], d_in.at[k], d_recv.at[k]).wait()
+
+    decays = d_in[...].reshape(CH, 128).T
+    state = s_in[0].astype(F32)
+    for k in range(1, CH - 1):
+        state = state * decays[:, k : k + 1] + s_in[k].astype(F32)
+    full = attended[...] + dot3(carried_q[...], state)
+    square = jnp.mean(full * full, axis=-1, keepdims=True)
+    norm_own[...] = (full * lax.rsqrt(square + 1e-06) * gain_row).astype(BF)
+    to_owners(norm_own, norm_in, norm_sem)
+    wait_bytes(gate_in.at[pl.ds(0, CH - 1)], gate_sem.at[1])
+    silu = gate_in[...].reshape(ROWS, 128)
+    wait_bytes(norm_in.at[pl.ds(0, CH - 1)], norm_sem.at[1])
+    normed = norm_in[...].reshape(ROWS, 128).astype(F32)
+    mixed = dot(mix[...], norm_in[...].reshape(ROWS, 128))
+    gat[M] = ((normed + mixed * inv_partners[...]) * silu).astype(BF)
 
     half = ROWS // 2
 
@@ -395,12 +445,26 @@
     last_store = pltpu.make_async_copy(grad_v, grad, out_sem.at[1])
     last_store.start()
 
-    wait_bytes(pack.at[pl.ds(0, TM - 1)], a_send)
+    for d in range(NX):
+        @pl.when(place == 0)
+        def _():
+            wait_bytes(rx.at[d, pl.ds(0, CH - 1)], a_send)
+
+        @pl.when(place != 0)
+        def _():
+            wait_bytes(rx.at[d], a_send)
+
+    wait_bytes(res_in.at[pl.ds(0, CH - 1)], r_sem.at[0])
     for one in pending:
         one.wait_send()
-    wait_bytes(d_in.at[pl.ds(0, TM - 1)], dk_sem.at[0])
-    wait_bytes(sbuf.at[pl.ds(0, TM - 1)], st_sem.at[0])
-    wait_bytes(pre.at[pl.ds(0, TM - 1)], p_send)
+    for k in range(1, CH):
+        @pl.when(span + k < CH)
+        def _():
+            for one in to_span(k):
+                one.wait_send()
+
+    wait_bytes(gate_in.at[pl.ds(0, CH - 1)], gate_sem.at[0])
+    wait_bytes(norm_in.at[pl.ds(0, CH - 1)], norm_sem.at[0])
     wait_bytes(xr.at[pl.ds(0, NX - 1)], x_sem.at[0])
     wait_bytes(zbuf.at[pl.ds(0, NZ - 1)], z_sem.at[0])
     store.wait()
@@ -413,26 +477,25 @@
 ):
     features = jnp.swapaxes(observations[0], 0, 1)
     weights = [
-        w.reshape(8, MP, 2, 16, 128) for w in (q_weight, k_weight, v_weight, decay_weight, gate_weight)
+        w.reshape(8, MP, 32, 128) for w in (q_weight, k_weight, v_weight, decay_weight, gate_weight)
     ]
     vm = pltpu.VMEM
     dma = pltpu.SemaphoreType.DMA
     scratch = [
-        vm((32, 4096), BF), vm((FR, CH), jnp.int32), vm((CH, FR), jnp.int32),
-        vm((MP, 2, 8, 16, 640), BF), vm((1, 128), F32), vm((1, 128), F32),
-        vm((MP, 128, 256), BF), vm((ROWS, 256), BF),
-        vm((TM, 16, 128), BF), vm((TM, 16, 128), BF), vm((MP, ROWS, 256), BF),
-        vm((ROWS, 640), F32), vm((ROWS, 128), F32), vm((CH, FR, 128), F32), vm((CH, 1, FR), F32),
+        vm((FR, CH), jnp.int32), vm((CH, FR), jnp.int32), vm((MP, 8, 32, 640), BF), vm((1, 128), F32),
+        vm((1, 128), F32), vm((MP, 128, 256), BF), vm((ROWS, 256), BF),
+        vm((NX, CH, 32, WAVE), BF), vm((MP, ROWS, 256), BF), vm((ROWS, 640), F32), vm((ROWS, 128), F32),
+        vm((CH, 1, 128), F32), vm((CH, 1, 128), F32), vm((CH, FR, 128), F32), vm((CH, 1, FR), F32),
         vm((len(LEVELS) + 1, FR, FR), F32), vm((len(LEVELS) * FR, FR), BF),
         vm((ROWS, ROWS), BF), vm((ROWS, 128), F32),
-        vm((TM, 16, 128), BF), vm((CH, 1, 128), F32), vm((TM, 16, 128), BF), vm((TM, 1, 128), F32),
-        vm((128, TM), F32), vm((TM, 16, 128), BF), vm((TM, 16, 128), BF),
-        vm((ROWS, 128), F32), vm((ROWS, 128), F32), vm((ROWS, 128), F32),
+        vm((CH, 128, 128), F32), vm((CH, 1, 128), F32), vm((128, 128), BF), vm((1, 128), F32),
+        vm((CH, 128, 128), BF), vm((CH, 1, 128), F32), vm((ROWS, 128), F32), vm((ROWS, 128), F32),
+        vm((ROWS, 128), F32), vm((CH, FR, 128), F32), vm((ROWS, 128), BF), vm((CH, FR, 128), BF),
         vm((MP, ROWS, 128), BF), vm((ROWS, 256), F32), vm((MP, 8, 16, 256), F32),
         vm((MP, 8, 16, 256), BF), vm((NX, 2, 8, 16, 256), BF), vm((NZ, 16, 256), F32),
         vm((NZ, 16, 256), BF), vm((NZ, 16, 256), BF), vm((ROWS, 256), BF), vm((16, 256), F32),
-        dma((7,)), dma, dma((2,)), dma, dma((NX,)), dma((NX, 7)), dma((NX, 7)), dma((2,)), dma((2,)), dma, dma((NX,)),
-        dma((14,)), dma((14,)), dma((2,)), dma((2,)),
+        dma((6,)), dma, dma((2,)), dma, dma((NX,)), dma((NX, 7)), dma((NX, 7)), dma((2,)),
+        dma((CH,)), dma((CH,)), dma((CH,)), dma((CH,)), dma((2,)), dma((2,)), dma((14,)), dma((14,)), dma((2,)), dma((2,)),
     ]
     following, weight_grad = pl.pallas_call(
         kernel,

time: 115 us -> 126 us (1.096)
  the two profiles are of different devices: /device:TPU:26 before, /device:TPU:16 now
where the time goes in v3:
time: 126 us
  Pallas kernels  123 us (98%)
  local copies, waits for them, and re-layouts  2.28 us (2%)
    pallas_call x1, Pallas kernels, local(): pl.pallas_call(kernel, out_shape=(jax.ShapeDtypeStruct((ROWS, 256), BF),...  123 us

profile of v3, /device:TPU:16, one launch (start us, length us, event | category | flops | bytes accessed | tf_op | source)
XLA Modules:
  0.0 125.7 jit_solution(1091047897033314193)
XLA Ops:
  0.6 122.8 %shard_map.131 = (bf16[512,256]{1,0:T(8,128)(2,1)}, f32[16,256]{1,0:T(8,128)}) custom-call(bf16[32,4096]{1,0:T(8,128)(2,1)} %bitcast.18, s32[64,8]{1,0:T(8,128)} %bitcast.21, s32[8,64]{1,0:T(8,128)} %resets.1, bf16[8,8,32,128]{3,2,1,0:T(8,128)(2,1)} %bitcast.12, bf16[8,8,32,128]{3,2,1,0:T(8,128)(2,1)} %bitcast.13, bf16[8,8,32,128]{3,2,1,0:T(8,128)(2,1)} %bitcast.14, ...), custom_call_target="tpu_custom_call" | custom-call | tf_op jit(solution)/shard_map/pallas_call | solution.py:500
  123.4 0.0 copy-start
  123.4 1.7 %copy.16 = bf16[8,64,256]{2,1,0:T(8,128)(2,1)} copy(bf16[8,64,256]{2,1,0:T(8,128)(2,1)} %bitcast.20) | data formatting | bytes 524288
  125.1 0.0 copy-done
  125.1 0.6 copy.17
Async XLA Ops:
  123.4 1.7 %copy-start = (f32[16,256]{1,0:T(8,128)S(1)}, f32[16,256]{1,0:T(8,128)}, u32[]{:S(2)}) copy-start(f32[16,256]{1,0:T(8,128)} %get-tuple-element.9) | copy-start | bytes 49156

commit v4 on v3

--- a/solution.py
+++ b/solution.py
@@ -48,10 +48,10 @@
     out, grad,
     con_v, res_v, w_v, bias_v, gain_v, ow_v, cot_v,
     rx, feat, proj, decay_log, res_own, res_in, rcol, rrow, masks, sel, mix, inv_partners,
-    local_state, before, s_own, d_own, s_in, d_in, attended, carried_q,
+    local_state, before, s_last, s_own, d_own, s_pair, d_pair, s_row, d_row, s_in, d_in, attended, carried_q,
     gate_own, gate_in, norm_own, norm_in,
     gat, oacc, gradf, gbuf, xr, zf, zbuf, zr, out_v, grad_v,
-    in_sem, w_sem, out_sem, a_send, a_recv, f_send, f_recv, r_sem, s_send, s_recv, d_send, d_recv,
+    in_sem, w_sem, out_sem, a_send, a_recv, f_send, f_recv, r_sem, e_send, e_recv, s_send, s_recv, d_send, d_recv,
     gate_sem, norm_sem, g_send, g_recv, x_sem, z_sem,
 ):
     T = lax.axis_index("tm")
@@ -59,10 +59,16 @@
     x, z = T // NZ, lax.rem(T, NZ)
     y, core = M // 2, lax.rem(M, 2)
     span, place = T // CH, lax.rem(T, CH)
-    char = lax.rem(place + span, CH)
+    half_row = lax.rem(span, 2)
+    at_home = lax.rem(span + 2 * x, CH) == place
+
+    def held(at):
+        return lax.rem(at + CH - 2 * x, CH)
+
+    char = held(place)
 
     def holder(other_span, other_char):
-        return other_span * CH + lax.rem(other_char - other_span + CH, CH)
+        return other_span * CH + lax.rem(other_char + 2 * (other_span // 2), CH)
 
     right_y, left_y, opp_y = lax.rem(y + 1, NY), lax.rem(y + 3, NY), lax.rem(y + 2, NY)
 
@@ -134,14 +140,14 @@
                     device_id=(peer, M), device_id_type=MESH,
                 ).start()
 
-        @pl.when(place == 0)
+        @pl.when(at_home)
         def _():
             pltpu.make_async_copy(quarter(span, d), rx.at[d, place], a_recv.at[d]).start()
 
     @pl.loop(1, CH)
     def _(k):
         to = lax.rem(place + k, CH)
-        piece(res_own.at[lax.rem(to + span, CH)], res_in.at[place], r_sem, span * CH + to).start()
+        piece(res_own.at[held(to)], res_in.at[place], r_sem, span * CH + to).start()
 
     for one in loads[1:]:
         one.wait()
@@ -166,9 +172,9 @@
     inv_partners[...] = 1.0 / jnp.maximum(dot(taken, jnp.ones((CH, 128), BF)), 1.0)
     spread = (iota((CH, ROWS), 1) // FR == iota((CH, ROWS), 0)).astype(BF)
     same = iota((ROWS, ROWS), 0) % FR == iota((ROWS, ROWS), 1) % FR
-    @pl.loop(0, CH)
+    @pl.loop(0, NX)
     def _(k):
-        @pl.when(k >= span)
+        @pl.when(k >= x)
         def _():
             s_in[k] = jnp.zeros((128, 128), BF)
             d_in[k] = jnp.ones((1, 128), F32)
@@ -254,56 +260,38 @@
                 local_state[s + 1] = after
                 before[s + 1] = product
             else:
+                s_last[...] = after
                 s_own[...] = after.astype(BF)
                 d_own[...] = product
 
-    def gates(d):
-        gate = proj[wave_rows(d), 512:640]
-        gate_own[wave_rows(d)] = gate / (1.0 + jnp.exp(-gate))
-        for s in (2 * d, 2 * d + 1):
-            @pl.when(s != place)
-            def _():
-                piece(gate_own.at[pl.ds(s * FR, FR)], gate_in.at[char], gate_sem, span * CH + s).start()
-
     own_features(0)
     own_features(1)
+    own_features(2)
     pass_on(0)
+    own_features(3)
+    pass_on(1)
     pass_opposite(0)
+    pass_on(2)
+    pass_opposite(1)
+    pass_on(3)
+    pass_opposite(2)
     project(0)
-    states(0)
-    gates(0)
-    own_features(2)
-    pass_on(1)
-    pass_opposite(1)
-    project(1)
-    states(1)
-    gates(1)
-    own_features(3)
-    pass_on(2)
-    pass_opposite(2)
-    pass_on(3)
-    project(2)
-    states(2)
-    gates(2)
     pass_opposite(3)
-    project(3)
-    states(3)
-
-    def to_span(k):
-        peer = holder(lax.rem(span + k, CH), char)
-        return [
-            pltpu.make_async_remote_copy(
-                src_ref=src, dst_ref=dst.at[span], send_sem=sent.at[k], recv_sem=recv.at[span],
-                device_id=(peer, M), device_id_type=MESH,
-            )
-            for src, dst, sent, recv in ((s_own, s_in, s_send, s_recv), (d_own, d_in, d_send, d_recv))
-        ]
-
-    for k in range(1, CH):
-        @pl.when(span + k < CH)
-        def _():
-            for one in to_span(k):
-                one.start()
+    for d in range(NX):
+        if d > 0:
+            project(d)
+        states(d)
+
+    def exchange(i, src, dst, peer):
+        return pltpu.make_async_remote_copy(
+            src_ref=src, dst_ref=dst, send_sem=e_send.at[i], recv_sem=e_recv.at[i],
+            device_id=(peer, M), device_id_type=MESH,
+        )
+
+    other = holder(span + 1 - 2 * half_row, char)
+    swap = [exchange(0, s_own, s_pair, other), exchange(1, d_own, d_pair, other)]
+    for one in swap:
+        one.start()
 
     def to_owners(src, dst, sems):
         @pl.loop(1, CH)
@@ -314,8 +302,34 @@
 
         dst[char] = src[pl.ds(pl.multiple_of(place * FR, FR), FR)]
 
-    gates(3)
-    gate_in[char] = gate_own[pl.ds(pl.multiple_of(place * FR, FR), FR)]
+    for one in swap:
+        one.wait_recv()
+    upper = half_row == 1
+    mine, theirs = s_last[...], s_pair[...].astype(F32)
+    my_decay, their_decay = d_own[...], d_pair[...]
+    late_decay = column(jnp.where(upper, my_decay, their_decay))
+    s_row[...] = (late_decay * jnp.where(upper, theirs, mine) + jnp.where(upper, mine, theirs)).astype(BF)
+    d_row[...] = my_decay * their_decay
+
+    def to_row(k):
+        peer = holder(lax.rem(span + 2 * k, CH), char)
+        return [
+            pltpu.make_async_remote_copy(
+                src_ref=src, dst_ref=dst.at[x], send_sem=sent.at[k], recv_sem=recv.at[x],
+                device_id=(peer, M), device_id_type=MESH,
+            )
+            for src, dst, sent, recv in ((s_row, s_in, s_send, s_recv), (d_row, d_in, d_send, d_recv))
+        ]
+
+    for k in range(1, NX):
+        @pl.when(x + k < NX)
+        def _():
+            for one in to_row(k):
+                one.start()
+
+    gate = proj[:, 512:640]
+    gate_own[...] = (gate / (1.0 + jnp.exp(-gate))).astype(BF)
+    to_owners(gate_own, gate_in, gate_sem)
 
     @pl.loop(0, CH)
     def _(c):
@@ -335,22 +349,22 @@
         scores = jnp.where(seen[:, :FR] == rrow[c], scores, 0.0)
         attended[rows, :] = dot3(scores, values) + dot3(carried, local_state[c])
 
-    for k in range(CH - 1):
-        @pl.when(k < span)
+    for k in range(NX - 1):
+        @pl.when(k < x)
         def _():
             pltpu.make_async_copy(s_in.at[k], s_in.at[k], s_recv.at[k]).wait()
             pltpu.make_async_copy(d_in.at[k], d_in.at[k], d_recv.at[k]).wait()
 
-    decays = d_in[...].reshape(CH, 128).T
     state = s_in[0].astype(F32)
-    for k in range(1, CH - 1):
-        state = state * decays[:, k : k + 1] + s_in[k].astype(F32)
+    for k in range(1, NX - 1):
+        state = state * column(d_in[k]) + s_in[k].astype(F32)
+    state = jnp.where(upper, state * column(d_pair[...]) + s_pair[...].astype(F32), state)
     full = attended[...] + dot3(carried_q[...], state)
     square = jnp.mean(full * full, axis=-1, keepdims=True)
     norm_own[...] = (full * lax.rsqrt(square + 1e-06) * gain_row).astype(BF)
     to_owners(norm_own, norm_in, norm_sem)
     wait_bytes(gate_in.at[pl.ds(0, CH - 1)], gate_sem.at[1])
-    silu = gate_in[...].reshape(ROWS, 128)
+    silu = gate_in[...].reshape(ROWS, 128).astype(F32)
     wait_bytes(norm_in.at[pl.ds(0, CH - 1)], norm_sem.at[1])
     normed = norm_in[...].reshape(ROWS, 128).astype(F32)
     mixed = dot(mix[...], norm_in[...].reshape(ROWS, 128))
@@ -446,21 +460,23 @@
     last_store.start()
 
     for d in range(NX):
-        @pl.when(place == 0)
+        @pl.when(at_home)
         def _():
             wait_bytes(rx.at[d, pl.ds(0, CH - 1)], a_send)
 
-        @pl.when(place != 0)
+        @pl.when(jnp.logical_not(at_home))
         def _():
             wait_bytes(rx.at[d], a_send)
 
     wait_bytes(res_in.at[pl.ds(0, CH - 1)], r_sem.at[0])
     for one in pending:
         one.wait_send()
-    for k in range(1, CH):
-        @pl.when(span + k < CH)
-        def _():
-            for one in to_span(k):
+    for one in swap:
+        one.wait_send()
+    for k in range(1, NX):
+        @pl.when(x + k < NX)
+        def _():
+            for one in to_row(k):
                 one.wait_send()
 
     wait_bytes(gate_in.at[pl.ds(0, CH - 1)], gate_sem.at[0])
@@ -488,14 +504,15 @@
         vm((CH, 1, 128), F32), vm((CH, 1, 128), F32), vm((CH, FR, 128), F32), vm((CH, 1, FR), F32),
         vm((len(LEVELS) + 1, FR, FR), F32), vm((len(LEVELS) * FR, FR), BF),
         vm((ROWS, ROWS), BF), vm((ROWS, 128), F32),
-        vm((CH, 128, 128), F32), vm((CH, 1, 128), F32), vm((128, 128), BF), vm((1, 128), F32),
-        vm((CH, 128, 128), BF), vm((CH, 1, 128), F32), vm((ROWS, 128), F32), vm((ROWS, 128), F32),
-        vm((ROWS, 128), F32), vm((CH, FR, 128), F32), vm((ROWS, 128), BF), vm((CH, FR, 128), BF),
+        vm((CH, 128, 128), F32), vm((CH, 1, 128), F32), vm((128, 128), F32),
+        vm((128, 128), BF), vm((1, 128), F32), vm((128, 128), BF), vm((1, 128), F32),
+        vm((128, 128), BF), vm((1, 128), F32), vm((NX, 128, 128), BF), vm((NX, 1, 128), F32), vm((ROWS, 128), F32), vm((ROWS, 128), F32),
+        vm((ROWS, 128), BF), vm((CH, FR, 128), BF), vm((ROWS, 128), BF), vm((CH, FR, 128), BF),
         vm((MP, ROWS, 128), BF), vm((ROWS, 256), F32), vm((MP, 8, 16, 256), F32),
         vm((MP, 8, 16, 256), BF), vm((NX, 2, 8, 16, 256), BF), vm((NZ, 16, 256), F32),
         vm((NZ, 16, 256), BF), vm((NZ, 16, 256), BF), vm((ROWS, 256), BF), vm((16, 256), F32),
         dma((6,)), dma, dma((2,)), dma, dma((NX,)), dma((NX, 7)), dma((NX, 7)), dma((2,)),
-        dma((CH,)), dma((CH,)), dma((CH,)), dma((CH,)), dma((2,)), dma((2,)), dma((14,)), dma((14,)), dma((2,)), dma((2,)),
+        dma((2,)), dma((2,)), dma((NX,)), dma((NX,)), dma((NX,)), dma((NX,)), dma((2,)), dma((2,)), dma((14,)), dma((14,)), dma((2,)), dma((2,)),
     ]
     following, weight_grad = pl.pallas_call(
         kernel,

time: 126 us -> 107 us (0.85)
  Pallas kernels: 123 us -> 104 us
    pallas_call x1, Pallas kernels: 123 us -> 104 us  [local(): pl.pallas_call(kernel, out_shape=(jax.ShapeDtypeStruct((ROWS, 256), BF),...]
where the time goes in v4:
time: 107 us
  Pallas kernels  104 us (97%)
  local copies, waits for them, and re-layouts  2.28 us (2%)
    pallas_call x1, Pallas kernels, local(): pl.pallas_call(kernel, out_shape=(jax.ShapeDtypeStruct((ROWS, 256), BF),...  104 us
    unnamed x4, local copies, waits for them, and re-layouts  2.28 us

profile of v4, /device:TPU:16, one launch (start us, length us, event | category | flops | bytes accessed | tf_op | source)
XLA Modules:
  0.0 107.1 jit_solution(14180429003906217704)
XLA Ops:
  0.6 104.2 %shard_map.131 = (bf16[512,256]{1,0:T(8,128)(2,1)}, f32[16,256]{1,0:T(8,128)}) custom-call(bf16[32,4096]{1,0:T(8,128)(2,1)} %bitcast.18, s32[64,8]{1,0:T(8,128)} %bitcast.21, s32[8,64]{1,0:T(8,128)} %resets.1, bf16[8,8,32,128]{3,2,1,0:T(8,128)(2,1)} %bitcast.12, bf16[8,8,32,128]{3,2,1,0:T(8,128)(2,1)} %bitcast.13, bf16[8,8,32,128]{3,2,1,0:T(8,128)(2,1)} %bitcast.14, ...), custom_call_target="tpu_custom_call" | custom-call | tf_op jit(solution)/shard_map/pallas_call | solution.py:517
  104.8 0.0 copy-start
  104.8 1.7 %copy.16 = bf16[8,64,256]{2,1,0:T(8,128)(2,1)} copy(bf16[8,64,256]{2,1,0:T(8,128)(2,1)} %bitcast.20) | data formatting | bytes 524288
  106.5 0.0 copy-done
  106.5 0.6 copy.17
Async XLA Ops:
  104.8 1.7 %copy-start = (f32[16,256]{1,0:T(8,128)S(1)}, f32[16,256]{1,0:T(8,128)}, u32[]{:S(2)}) copy-start(f32[16,256]{1,0:T(8,128)} %get-tuple-element.9) | copy-start | bytes 49156

commit v5 on v4

--- a/solution.py
+++ b/solution.py
@@ -52,7 +52,7 @@
     gate_own, gate_in, norm_own, norm_in,
     gat, oacc, gradf, gbuf, xr, zf, zbuf, zr, out_v, grad_v,
     in_sem, w_sem, out_sem, a_send, a_recv, f_send, f_recv, r_sem, e_send, e_recv, s_send, s_recv, d_send, d_recv,
-    gate_sem, norm_sem, g_send, g_recv, x_sem, z_sem,
+    gate_sem, norm_sem, g_send, g_recv, x_send, x_recv, z_sem,
 ):
     T = lax.axis_index("tm")
     M = lax.axis_index("mp")
@@ -282,57 +282,12 @@
             project(d)
         states(d)
 
-    def exchange(i, src, dst, peer):
-        return pltpu.make_async_remote_copy(
-            src_ref=src, dst_ref=dst, send_sem=e_send.at[i], recv_sem=e_recv.at[i],
-            device_id=(peer, M), device_id_type=MESH,
-        )
-
-    other = holder(span + 1 - 2 * half_row, char)
-    swap = [exchange(0, s_own, s_pair, other), exchange(1, d_own, d_pair, other)]
-    for one in swap:
-        one.start()
-
-    def to_owners(src, dst, sems):
-        @pl.loop(1, CH)
-        def _(k):
-            to = lax.rem(place + k, CH)
-            rows = pl.ds(pl.multiple_of(to * FR, FR), FR)
-            piece(src.at[rows], dst.at[char], sems, span * CH + to).start()
-
-        dst[char] = src[pl.ds(pl.multiple_of(place * FR, FR), FR)]
-
-    for one in swap:
-        one.wait_recv()
-    upper = half_row == 1
-    mine, theirs = s_last[...], s_pair[...].astype(F32)
-    my_decay, their_decay = d_own[...], d_pair[...]
-    late_decay = column(jnp.where(upper, my_decay, their_decay))
-    s_row[...] = (late_decay * jnp.where(upper, theirs, mine) + jnp.where(upper, mine, theirs)).astype(BF)
-    d_row[...] = my_decay * their_decay
-
-    def to_row(k):
-        peer = holder(lax.rem(span + 2 * k, CH), char)
-        return [
-            pltpu.make_async_remote_copy(
-                src_ref=src, dst_ref=dst.at[x], send_sem=sent.at[k], recv_sem=recv.at[x],
-                device_id=(peer, M), device_id_type=MESH,
-            )
-            for src, dst, sent, recv in ((s_row, s_in, s_send, s_recv), (d_row, d_in, d_send, d_recv))
-        ]
-
-    for k in range(1, NX):
-        @pl.when(x + k < NX)
-        def _():
-            for one in to_row(k):
-                one.start()
-
-    gate = proj[:, 512:640]
-    gate_own[...] = (gate / (1.0 + jnp.exp(-gate))).astype(BF)
-    to_owners(gate_own, gate_in, gate_sem)
-
-    @pl.loop(0, CH)
-    def _(c):
+    def inside(low, high):
+        @pl.loop(low, high)
+        def _(c):
+            inside_one(c)
+
+    def inside_one(c):
         rows = pl.ds(pl.multiple_of(c * FR, FR), FR)
         total = decay_log[rows, :]
         queries = proj[rows, 0:128] * HK ** (-0.5)
@@ -349,6 +304,59 @@
         scores = jnp.where(seen[:, :FR] == rrow[c], scores, 0.0)
         attended[rows, :] = dot3(scores, values) + dot3(carried, local_state[c])
 
+    def exchange(i, src, dst, peer):
+        return pltpu.make_async_remote_copy(
+            src_ref=src, dst_ref=dst, send_sem=e_send.at[i], recv_sem=e_recv.at[i],
+            device_id=(peer, M), device_id_type=MESH,
+        )
+
+    other = holder(span + 1 - 2 * half_row, char)
+    swap = [exchange(0, s_own, s_pair, other), exchange(1, d_own, d_pair, other)]
+    for one in swap:
+        one.start()
+
+    inside(0, 6)
+    gate = proj[:, 512:640]
+    gate_own[...] = (gate / (1.0 + jnp.exp(-gate))).astype(BF)
+
+    def to_owners(src, dst, sems):
+        @pl.loop(1, CH)
+        def _(k):
+            to = lax.rem(place + k, CH)
+            rows = pl.ds(pl.multiple_of(to * FR, FR), FR)
+            piece(src.at[rows], dst.at[char], sems, span * CH + to).start()
+
+        dst[char] = src[pl.ds(pl.multiple_of(place * FR, FR), FR)]
+
+    for one in swap:
+        one.wait_recv()
+    upper = half_row == 1
+    mine, theirs = s_last[...], s_pair[...].astype(F32)
+    my_decay, their_decay = d_own[...], d_pair[...]
+    late_decay = column(jnp.where(upper, my_decay, their_decay))
+    s_row[...] = (late_decay * jnp.where(upper, theirs, mine) + jnp.where(upper, mine, theirs)).astype(BF)
+    d_row[...] = my_decay * their_decay
+
+    def to_row(k):
+        peer = holder(lax.rem(span + 2 * k, CH), char)
+        return [
+            pltpu.make_async_remote_copy(
+                src_ref=src, dst_ref=dst.at[x], send_sem=sent.at[k], recv_sem=recv.at[x],
+                device_id=(peer, M), device_id_type=MESH,
+            )
+            for src, dst, sent, recv in ((s_row, s_in, s_send, s_recv), (d_row, d_in, d_send, d_recv))
+        ]
+
+    for k in range(1, NX):
+        @pl.when(x + k < NX)
+        def _():
+            for one in to_row(k):
+                one.start()
+
+    to_owners(gate_own, gate_in, gate_sem)
+
+    inside(6, CH)
+
     for k in range(NX - 1):
         @pl.when(k < x)
         def _():
@@ -385,18 +393,25 @@
     def arrived(slot, h, i):
         gated_part(slot, h, i, sib).wait_recv()
 
+    def along_x(m):
+        to, j = m // 2, lax.rem(m, 2)
+        return pltpu.make_async_remote_copy(
+            src_ref=gbuf.at[m], dst_ref=xr.at[j, x], send_sem=x_send, recv_sem=x_recv.at[j],
+            device_id=(to * NZ + z, M), device_id_type=MESH,
+        )
+
     def produce(m, first=False):
         rows = gat[m]
-        term = dot(rows, ow_v[m])
-        oacc[...] = term if first else oacc[...] + term
         part = dot(rows, cot_v[...], ((0,), (0,))).reshape(8, 16, 256)
         gradf[m] = part
         gbuf[m] = part.astype(BF)
 
-    def along_x(to):
-        @pl.when(to != x)
-        def _():
-            piece(gbuf.at[pl.ds(2 * to, 2)], xr.at[x], x_sem, to * NZ + z).start()
+        @pl.when(m // 2 != x)
+        def _():
+            along_x(m).start()
+
+        term = dot(rows, ow_v[m])
+        oacc[...] = term if first else oacc[...] + term
 
     go(M, 0, 2, right)
     go(M, 1, 5, left)
@@ -413,43 +428,44 @@
     go(right, 1, 11, sib)
     arrived(sib, 0, 0)
     arrived(sib, 1, 1)
-    produce(sib)
-    along_x(y)
     arrived(left, 1, 3)
     go(left, 1, 9, sib)
     arrived(right, 0, 4)
     go(right, 0, 10, sib)
     produce(left)
+    produce(right)
     arrived(opp, 0, 6)
     go(opp, 0, 12, sib)
     arrived(opp, 1, 7)
     go(opp, 1, 13, sib)
-    produce(right)
+    produce(opp)
+    produce(sib)
     for yy, i in ((left_y, 8), (right_y, 10), (opp_y, 12)):
         slot = 2 * yy + 1 - core
         arrived(slot, 0, i)
         arrived(slot, 1, i + 1)
-        if i == 12:
-            produce(opp)
         produce(slot)
-        along_x(yy)
 
     out_v[...] = oacc[...].astype(BF)
     store = pltpu.make_async_copy(out_v, out, out_sem.at[0])
     store.start()
 
-    wait_bytes(xr.at[pl.ds(0, NX - 1)], x_sem.at[1])
-    total = gradf[pl.ds(2 * x, 2)]
-    for d in range(1, NX):
-        total += xr[lax.rem(x + d, NX)].astype(F32)
-    total = total.reshape(NZ, 16, 256)
-    zf[...] = total
-    zbuf[...] = total.astype(BF)
-
-    @pl.loop(1, NZ)
-    def _(k):
-        to = lax.rem(z + k, NZ)
-        piece(zbuf.at[to], zr.at[z], z_sem, x * NZ + to).start()
+    for j in (core, 1 - core):
+        wait_bytes(xr.at[j, pl.ds(0, NX - 1)], x_recv.at[j])
+        total = gradf[2 * x + j]
+        for d in range(1, NX):
+            total += xr[j, lax.rem(x + d, NX)].astype(F32)
+        owners = pl.ds(j * 8, 8)
+        zf[owners] = total
+        zbuf[owners] = total.astype(BF)
+
+        @pl.loop(0, 8)
+        def _(k):
+            to = j * 8 + lax.rem(z + k, 8)
+
+            @pl.when(to != z)
+            def _():
+                piece(zbuf.at[to], zr.at[z], z_sem, x * NZ + to).start()
 
     wait_bytes(zr.at[pl.ds(0, NZ - 1)], z_sem.at[1])
     total = zf[z]
@@ -481,7 +497,8 @@
 
     wait_bytes(gate_in.at[pl.ds(0, CH - 1)], gate_sem.at[0])
     wait_bytes(norm_in.at[pl.ds(0, CH - 1)], norm_sem.at[0])
-    wait_bytes(xr.at[pl.ds(0, NX - 1)], x_sem.at[0])
+    for j in range(2):
+        wait_bytes(xr.at[j, pl.ds(0, NX - 1)], x_send)
     wait_bytes(zbuf.at[pl.ds(0, NZ - 1)], z_sem.at[0])
     store.wait()
     last_store.wait()
@@ -509,10 +526,10 @@
         vm((128, 128), BF), vm((1, 128), F32), vm((NX, 128, 128), BF), vm((NX, 1, 128), F32), vm((ROWS, 128), F32), vm((ROWS, 128), F32),
         vm((ROWS, 128), BF), vm((CH, FR, 128), BF), vm((ROWS, 128), BF), vm((CH, FR, 128), BF),
         vm((MP, ROWS, 128), BF), vm((ROWS, 256), F32), vm((MP, 8, 16, 256), F32),
-        vm((MP, 8, 16, 256), BF), vm((NX, 2, 8, 16, 256), BF), vm((NZ, 16, 256), F32),
+        vm((MP, 8, 16, 256), BF), vm((2, NX, 8, 16, 256), BF), vm((NZ, 16, 256), F32),
         vm((NZ, 16, 256), BF), vm((NZ, 16, 256), BF), vm((ROWS, 256), BF), vm((16, 256), F32),
         dma((6,)), dma, dma((2,)), dma, dma((NX,)), dma((NX, 7)), dma((NX, 7)), dma((2,)),
-        dma((2,)), dma((2,)), dma((NX,)), dma((NX,)), dma((NX,)), dma((NX,)), dma((2,)), dma((2,)), dma((14,)), dma((14,)), dma((2,)), dma((2,)),
+        dma((2,)), dma((2,)), dma((NX,)), dma((NX,)), dma((NX,)), dma((NX,)), dma((2,)), dma((2,)), dma((14,)), dma((14,)), dma, dma((2,)), dma((2,)),
     ]
     following, weight_grad = pl.pallas_call(
         kernel,

time: 107 us -> 104 us (0.972)
  the two profiles are of different devices: /device:TPU:16 before, /device:TPU:49 now
where the time goes in v5:
time: 104 us
  Pallas kernels  101 us (97%)
  local copies, waits for them, and re-layouts  2.28 us (2%)
    pallas_call x1, Pallas kernels, local(): pl.pallas_call(kernel, out_shape=(jax.ShapeDtypeStruct((ROWS, 256), BF),...  101 us
    unnamed x4, local copies, waits for them, and re-layouts  2.28 us

profile of v5, /device:TPU:49, one launch (start us, length us, event | category | flops | bytes accessed | tf_op | source)
XLA Modules:
  0.0 103.9 jit_solution(1450183839748473162)
XLA Ops:
  0.6 101.0 %shard_map.131 = (bf16[512,256]{1,0:T(8,128)(2,1)}, f32[16,256]{1,0:T(8,128)}) custom-call(bf16[32,4096]{1,0:T(8,128)(2,1)} %bitcast.18, s32[64,8]{1,0:T(8,128)} %bitcast.21, s32[8,64]{1,0:T(8,128)} %resets.1, bf16[8,8,32,128]{3,2,1,0:T(8,128)(2,1)} %bitcast.12, bf16[8,8,32,128]{3,2,1,0:T(8,128)(2,1)} %bitcast.13, bf16[8,8,32,128]{3,2,1,0:T(8,128)(2,1)} %bitcast.14, ...), custom_call_target="tpu_custom_call" | custom-call | tf_op jit(solution)/shard_map/pallas_call | solution.py:534
  101.6 0.0 copy-start
  101.6 1.7 %copy.16 = bf16[8,64,256]{2,1,0:T(8,128)(2,1)} copy(bf16[8,64,256]{2,1,0:T(8,128)(2,1)} %bitcast.20) | data formatting | bytes 524288
  103.3 0.0 copy-done
  103.3 0.6 copy.17
Async XLA Ops:
  101.6 1.7 %copy-start = (f32[16,256]{1,0:T(8,128)S(1)}, f32[16,256]{1,0:T(8,128)}, u32[]{:S(2)}) copy-start(f32[16,256]{1,0:T(8,128)} %get-tuple-element.9) | copy-start | bytes 49156

commit v6 on v5

--- a/solution.py
+++ b/solution.py
@@ -264,6 +264,14 @@
                 s_own[...] = after.astype(BF)
                 d_own[...] = product
 
+    def gates(d):
+        gate = proj[wave_rows(d), 512:640]
+        gate_own[wave_rows(d)] = (gate / (1.0 + jnp.exp(-gate))).astype(BF)
+        for s in (2 * d, 2 * d + 1):
+            @pl.when(s != place)
+            def _():
+                piece(gate_own.at[pl.ds(s * FR, FR)], gate_in.at[char], gate_sem, span * CH + s).start()
+
     own_features(0)
     own_features(1)
     own_features(2)
@@ -276,11 +284,17 @@
     pass_on(3)
     pass_opposite(2)
     project(0)
+    gates(0)
     pass_opposite(3)
-    for d in range(NX):
-        if d > 0:
-            project(d)
-        states(d)
+    project(1)
+    gates(1)
+    states(0)
+    project(2)
+    gates(2)
+    states(1)
+    states(2)
+    project(3)
+    states(3)
 
     def inside(low, high):
         @pl.loop(low, high)
@@ -315,9 +329,9 @@
     for one in swap:
         one.start()
 
+    gates(3)
+    gate_in[char] = gate_own[pl.ds(pl.multiple_of(place * FR, FR), FR)]
     inside(0, 6)
-    gate = proj[:, 512:640]
-    gate_own[...] = (gate / (1.0 + jnp.exp(-gate))).astype(BF)
 
     def to_owners(src, dst, sems):
         @pl.loop(1, CH)
@@ -353,7 +367,6 @@
             for one in to_row(k):
                 one.start()
 
-    to_owners(gate_own, gate_in, gate_sem)
 
     inside(6, CH)
 

time: 104 us -> 104 us (level)
  the two profiles are of different devices: /device:TPU:49 before, /device:TPU:58 now
where the time goes in v6:
time: 104 us
  Pallas kernels  101 us (97%)
  local copies, waits for them, and re-layouts  2.28 us (2%)
    pallas_call x1, Pallas kernels, local(): pl.pallas_call(kernel, out_shape=(jax.ShapeDtypeStruct((ROWS, 256), BF),...  101 us
    unnamed x4, local copies, waits for them, and re-layouts  2.28 us

profile of v6, /device:TPU:58, one launch (start us, length us, event | category | flops | bytes accessed | tf_op | source)
XLA Modules:
  0.0 103.6 jit_solution(18325362362031749037)
XLA Ops:
  0.6 100.7 %shard_map.131 = (bf16[512,256]{1,0:T(8,128)(2,1)}, f32[16,256]{1,0:T(8,128)}) custom-call(bf16[32,4096]{1,0:T(8,128)(2,1)} %bitcast.18, s32[64,8]{1,0:T(8,128)} %bitcast.21, s32[8,64]{1,0:T(8,128)} %resets.1, bf16[8,8,32,128]{3,2,1,0:T(8,128)(2,1)} %bitcast.12, bf16[8,8,32,128]{3,2,1,0:T(8,128)(2,1)} %bitcast.13, bf16[8,8,32,128]{3,2,1,0:T(8,128)(2,1)} %bitcast.14, ...), custom_call_target="tpu_custom_call" | custom-call | tf_op jit(solution)/shard_map/pallas_call | solution.py:547
  101.3 0.0 copy-start
  101.3 1.7 %copy.16 = bf16[8,64,256]{2,1,0:T(8,128)(2,1)} copy(bf16[8,64,256]{2,1,0:T(8,128)(2,1)} %bitcast.20) | data formatting | bytes 524288
  103.0 0.0 copy-done
  103.0 0.6 copy.17
Async XLA Ops:
  101.3 1.7 %copy-start = (f32[16,256]{1,0:T(8,128)S(1)}, f32[16,256]{1,0:T(8,128)}, u32[]{:S(2)}) copy-start(f32[16,256]{1,0:T(8,128)} %get-tuple-element.9) | copy-start | bytes 49156

commit v7 on v6

--- a/solution.py
+++ b/solution.py
@@ -352,7 +352,10 @@
     d_row[...] = my_decay * their_decay
 
     def to_row(k):
-        peer = holder(lax.rem(span + 2 * k, CH), char)
+        if k == 2:
+            peer = holder(lax.rem(span + 4, CH), char)
+        else:
+            peer = lax.rem(x + k, NX) * NZ + lax.rem(z + (2 if k == 1 else NZ - 2), NZ)
         return [
             pltpu.make_async_remote_copy(
                 src_ref=src, dst_ref=dst.at[x], send_sem=sent.at[k], recv_sem=recv.at[x],

time: 104 us -> 103 us (level)
  the two profiles are of different devices: /device:TPU:58 before, /device:TPU:48 now
where the time goes in v7:
time: 103 us
  Pallas kernels  99.9 us (97%)
  local copies, waits for them, and re-layouts  2.28 us (2%)
    pallas_call x1, Pallas kernels, local(): pl.pallas_call(kernel, out_shape=(jax.ShapeDtypeStruct((ROWS, 256), BF),...  99.9 us
    unnamed x4, local copies, waits for them, and re-layouts  2.28 us

profile of v7, /device:TPU:48, one launch (start us, length us, event | category | flops | bytes accessed | tf_op | source)
XLA Modules:
  0.0 102.9 jit_solution(15913697608193776502)
XLA Ops:
  0.6 99.9 %shard_map.131 = (bf16[512,256]{1,0:T(8,128)(2,1)}, f32[16,256]{1,0:T(8,128)}) custom-call(bf16[32,4096]{1,0:T(8,128)(2,1)} %bitcast.18, s32[64,8]{1,0:T(8,128)} %bitcast.21, s32[8,64]{1,0:T(8,128)} %resets.1, bf16[8,8,32,128]{3,2,1,0:T(8,128)(2,1)} %bitcast.12, bf16[8,8,32,128]{3,2,1,0:T(8,128)(2,1)} %bitcast.13, bf16[8,8,32,128]{3,2,1,0:T(8,128)(2,1)} %bitcast.14, ...), custom_call_target="tpu_custom_call" | custom-call | tf_op jit(solution)/shard_map/pallas_call | solution.py:550
  100.6 0.0 copy-start
  100.6 1.7 %copy.16 = bf16[8,64,256]{2,1,0:T(8,128)(2,1)} copy(bf16[8,64,256]{2,1,0:T(8,128)(2,1)} %bitcast.20) | data formatting | bytes 524288
  102.2 0.0 copy-done
  102.3 0.6 copy.17
Async XLA Ops:
  100.6 1.7 %copy-start = (f32[16,256]{1,0:T(8,128)S(1)}, f32[16,256]{1,0:T(8,128)}, u32[]{:S(2)}) copy-start(f32[16,256]{1,0:T(8,128)} %get-tuple-element.9) | copy-start | bytes 49156

commit v8 on v7

--- a/solution.py
+++ b/solution.py
@@ -333,15 +333,6 @@
     gate_in[char] = gate_own[pl.ds(pl.multiple_of(place * FR, FR), FR)]
     inside(0, 6)
 
-    def to_owners(src, dst, sems):
-        @pl.loop(1, CH)
-        def _(k):
-            to = lax.rem(place + k, CH)
-            rows = pl.ds(pl.multiple_of(to * FR, FR), FR)
-            piece(src.at[rows], dst.at[char], sems, span * CH + to).start()
-
-        dst[char] = src[pl.ds(pl.multiple_of(place * FR, FR), FR)]
-
     for one in swap:
         one.wait_recv()
     upper = half_row == 1
@@ -383,10 +374,22 @@
     for k in range(1, NX - 1):
         state = state * column(d_in[k]) + s_in[k].astype(F32)
     state = jnp.where(upper, state * column(d_pair[...]) + s_pair[...].astype(F32), state)
-    full = attended[...] + dot3(carried_q[...], state)
-    square = jnp.mean(full * full, axis=-1, keepdims=True)
-    norm_own[...] = (full * lax.rsqrt(square + 1e-06) * gain_row).astype(BF)
-    to_owners(norm_own, norm_in, norm_sem)
+    for h in range(2):
+        rows = pl.ds(h * (ROWS // 2), ROWS // 2)
+        full = attended[rows, :] + dot3(carried_q[rows, :], state)
+        square = jnp.mean(full * full, axis=-1, keepdims=True)
+        norm_own[rows, :] = (full * lax.rsqrt(square + 1e-06) * gain_row).astype(BF)
+
+        @pl.loop(0, 4)
+        def _(k):
+            to = h * 4 + lax.rem(place + k, 4)
+
+            @pl.when(to != place)
+            def _():
+                sent_rows = norm_own.at[pl.ds(pl.multiple_of(to * FR, FR), FR)]
+                piece(sent_rows, norm_in.at[char], norm_sem, span * CH + to).start()
+
+    norm_in[char] = norm_own[pl.ds(pl.multiple_of(place * FR, FR), FR)]
     wait_bytes(gate_in.at[pl.ds(0, CH - 1)], gate_sem.at[1])
     silu = gate_in[...].reshape(ROWS, 128).astype(F32)
     wait_bytes(norm_in.at[pl.ds(0, CH - 1)], norm_sem.at[1])

time: 103 us -> 103 us (level)
  the two profiles are of different devices: /device:TPU:48 before, /device:TPU:58 now
where the time goes in v8:
time: 103 us
  Pallas kernels  99.6 us (97%)
  local copies, waits for them, and re-layouts  2.28 us (2%)
    pallas_call x1, Pallas kernels, local(): pl.pallas_call(kernel, out_shape=(jax.ShapeDtypeStruct((ROWS, 256), BF),...  99.6 us
    unnamed x4, local copies, waits for them, and re-layouts  2.28 us

profile of v8, /device:TPU:58, one launch (start us, length us, event | category | flops | bytes accessed | tf_op | source)
XLA Modules:
  0.0 102.6 jit_solution(2672616310515391127)
XLA Ops:
  0.6 99.6 %shard_map.131 = (bf16[512,256]{1,0:T(8,128)(2,1)}, f32[16,256]{1,0:T(8,128)}) custom-call(bf16[32,4096]{1,0:T(8,128)(2,1)} %bitcast.18, s32[64,8]{1,0:T(8,128)} %bitcast.21, s32[8,64]{1,0:T(8,128)} %resets.1, bf16[8,8,32,128]{3,2,1,0:T(8,128)(2,1)} %bitcast.12, bf16[8,8,32,128]{3,2,1,0:T(8,128)(2,1)} %bitcast.13, bf16[8,8,32,128]{3,2,1,0:T(8,128)(2,1)} %bitcast.14, ...), custom_call_target="tpu_custom_call" | custom-call | tf_op jit(solution)/shard_map/pallas_call | solution.py:553
  100.3 0.0 copy-start
  100.3 1.7 %copy.16 = bf16[8,64,256]{2,1,0:T(8,128)(2,1)} copy(bf16[8,64,256]{2,1,0:T(8,128)(2,1)} %bitcast.20) | data formatting | bytes 524288
  102.0 0.0 copy-done
  102.0 0.6 copy.17
Async XLA Ops:
  100.3 1.7 %copy-start = (f32[16,256]{1,0:T(8,128)S(1)}, f32[16,256]{1,0:T(8,128)}, u32[]{:S(2)}) copy-start(f32[16,256]{1,0:T(8,128)} %get-tuple-element.9) | copy-start | bytes 49156
